TPU v7x, 32 devices: a whole 2x2x4 slice. The times are simulated.
32 devices in a mesh: groups: 2 (over y), store: 4 (over z), tensor: 4 (over x, core).
Axes of the slice: x: 2, y: 2, z: 4, core: 2. Of those that a mesh axis runs over, the one named last changes fastest.
Arguments:
- stream: bfloat16 [1024, 4608], P(('groups', 'store')), parts along dimension 0, may hold values from -6 to 6
- input_norm_gain: bfloat16 [4608], replicated, may hold values from 0.5 to 1.5
- output_norm_gain: bfloat16 [4608], P('tensor'), may hold values from 0.5 to 1.5
- query_projection: bfloat16 [4608, 4096], P(None, 'tensor'), may hold values from -0.09375 to 0.09375
- key_value_weight: bfloat16 [4608, 2, 2048], P(None, None, 'tensor'), may hold values from -0.09375 to 0.09375
- output_projection: bfloat16 [4096, 4608], P('tensor'), may hold values from -0.09375 to 0.09375
- cached_key_value: bfloat16 [2, 1024, 16, 128, 128], P(None, ('groups', 'store'), 'tensor'), parts along dimension 1, may hold values from -900 to 900
- row_cache_length: int32 [1024], P(('groups', 'store')), parts along dimension 0, may hold values from 1 to 128, as said below
- row_adapter_index: int32 [1024], P(('groups', 'store')), parts along dimension 0, may hold values from 0 to 31, as said below
- adapter_slot_table: int32 [64], P('groups'), parts along dimension 0, may hold values from 0 to 31, as said below
- adapter_rank_table: int32 [64], P('groups'), parts along dimension 0, may hold values from 8 to 64, as said below
- adapter_down_weight: bfloat16 [4096, 64, 64], P('tensor', ('groups', 'store')), parts along dimension 1, may hold values from -0.09375 to 0.09375
- adapter_up_weight: bfloat16 [64, 64, 4608], P(('groups', 'store'), None, 'tensor'), parts along dimension 0, may hold values from -0.75 to 0.75
Outputs:
- updated: bfloat16 [1024, 4608], P(('groups', 'store'), 'tensor'), parts along dimension 0
There are 2 independent parts, one for each index of `groups`. A program takes and returns all parts, laid end to end along the dimension named above; an argument that names none is the same for every part. Nothing has to cross between parts.
Inputs may be any that keep to these rules, and one draw needn't show every extreme that they name: `row_adapter_index`: on the rows of one store index (aligned blocks of 128 rows), at most 32 rows name adapters whose slot lies in one owner's range (adapter_slot_table[id] // 8 == owner); in every draw one owner gets exactly 32 rows from every block. `adapter_slot_table`: A permutation of the slots. `adapter_rank_table`: factor entries at rank positions from this value on are padding. `row_cache_length`: positions below this are live; the new token sits at this position.
All inputs are finite; a program needn't handle non-finite values.
Results may differ from a plain program's by a relative error of at most 0.011.
Values may be sent and summed in bfloat16 or wider, within the bound.
A program may use at most 192 MiB of HBM per device.

v0:
```python
import math

import jax
import jax.numpy as jnp
from jax import lax
from jax.sharding import PartitionSpec as P

HEAD_WIDTH = 128


epsilon = 1e-06
adapter_strength = 32.0
query_factor = 144.0 ** (-0.5)
rope_base = 10000.0


def normed_rows(values, gain):
    mean = jnp.mean(values * values, axis=-1, keepdims=True)
    return values * lax.rsqrt(mean + epsilon) * gain


def rotate(values, position):
    half = values.shape[-1] // 2
    freq = jnp.exp(
        jnp.arange(half, dtype=jnp.float32) * (-2.0 * math.log(rope_base) / values.shape[-1])
    )
    angle = position.astype(jnp.float32)[:, None] * freq[None, :]
    cosine = jnp.cos(angle)[:, None, :]
    sine = jnp.sin(angle)[:, None, :]
    first = values[..., :half]
    second = values[..., half:]
    return jnp.concatenate(
        [first * cosine - second * sine, second * cosine + first * sine], axis=-1
    )


def attend(query, key_new, value_new, keys, values, row_cache_length):
    scores = (
        jnp.einsum("bgrd,bgld->bgrl", query, keys, preferred_element_type=jnp.float32)
        * query_factor
    )
    own = (
        jnp.einsum("bgrd,bgd->bgr", query, key_new, preferred_element_type=jnp.float32)
        * query_factor
    )
    valid = jnp.arange(keys.shape[2])[None, :] < row_cache_length[:, None]
    scores = jnp.where(valid[:, None, None, :], scores, -jnp.inf)
    top = jnp.maximum(jnp.max(scores, axis=-1), own)
    weights = jnp.exp(scores - top[..., None])
    own_weight = jnp.exp(own - top)
    total = jnp.sum(weights, axis=-1) + own_weight
    probs = (weights / total[..., None]).astype(jnp.bfloat16)
    own_prob = (own_weight / total).astype(jnp.bfloat16)
    mixed = jnp.einsum("bgrl,bgld->bgrd", probs, values, preferred_element_type=jnp.float32)
    mixed = (
        mixed
        + own_prob.astype(jnp.float32)[..., None] * value_new.astype(jnp.float32)[:, :, None, :]
    )
    return mixed.astype(jnp.bfloat16).reshape(query.shape[0], -1)


def per_device(
    stream,
    input_norm_gain,
    output_norm_gain,
    query_projection,
    key_value_weight,
    output_projection,
    cached_key_value,
    row_cache_length,
    row_adapter_index,
    adapter_slot_table,
    adapter_rank_table,
    adapter_down_weight,
    adapter_up_weight,
):
    stores = lax.axis_size("store")
    column = lax.axis_index("tensor")
    row_count, width = stream.shape
    kept_factors = adapter_down_weight.shape[1]
    rank_padding = adapter_down_weight.shape[2]
    adapter_portion = adapter_up_weight.shape[2]
    capacity = row_count // 4
    heads_local = query_projection.shape[1] // HEAD_WIDTH
    pairs_local = key_value_weight.shape[2] // HEAD_WIDTH
    stream_f = stream.astype(jnp.float32)
    normed = normed_rows(stream_f, input_norm_gain.astype(jnp.float32)).astype(jnp.bfloat16)
    query = jnp.dot(normed, query_projection, preferred_element_type=jnp.float32).reshape(
        row_count, heads_local, HEAD_WIDTH
    )
    query = rotate(query, row_cache_length).astype(jnp.bfloat16)
    query = query.reshape(row_count, pairs_local, heads_local // pairs_local, HEAD_WIDTH)
    pair = jnp.dot(normed, key_value_weight.reshape(width, -1), preferred_element_type=jnp.float32)
    pair = pair.reshape(row_count, 2, pairs_local, HEAD_WIDTH)
    key_new = rotate(pair[:, 0], row_cache_length).astype(jnp.bfloat16)
    value_new = pair[:, 1].astype(jnp.bfloat16)
    mixed = attend(
        query, key_new, value_new, cached_key_value[0], cached_key_value[1], row_cache_length
    )
    adapters = adapter_slot_table.shape[0]
    match = row_adapter_index[:, None] == jnp.arange(adapters)[None, :]
    slot = jnp.sum(jnp.where(match, adapter_slot_table[None, :], 0), axis=1)
    adapter_rank_value = jnp.sum(jnp.where(match, adapter_rank_table[None, :], 0), axis=1)
    owner = slot // kept_factors
    within = slot - owner * kept_factors
    target = (owner[:, None] == jnp.arange(stores)[None, :]).astype(jnp.int32)
    before = jnp.cumsum(target, axis=0) - target
    bucket = owner * capacity + jnp.sum(before * target, axis=1)
    packer = (bucket[None, :] == jnp.arange(stores * capacity)[:, None]).astype(jnp.bfloat16)
    outgoing = jnp.dot(packer, mixed, preferred_element_type=jnp.float32).astype(jnp.bfloat16)
    outgoing = outgoing.reshape(stores, capacity, -1)
    labels = jnp.stack(
        [(within + 1).astype(jnp.float32), adapter_rank_value.astype(jnp.float32)], axis=-1
    )
    labels = (
        jnp.dot(packer.astype(jnp.float32), labels)
        .astype(jnp.bfloat16)
        .reshape(stores, capacity, 2)
    )
    down_factor = adapter_down_weight.reshape(
        adapter_down_weight.shape[0], kept_factors * rank_padding
    )
    up_factor = adapter_up_weight.reshape(kept_factors * rank_padding, adapter_portion)
    block = lax.all_to_all(outgoing, "store", split_axis=0, concat_axis=0, tiled=True)
    marks = lax.all_to_all(labels, "store", split_axis=0, concat_axis=0, tiled=True)
    count = block.shape[0] * block.shape[1]
    flat = block.reshape(count, -1)
    code = marks[..., 0].reshape(count).astype(jnp.float32)
    row_rank_value = marks[..., 1].reshape(count).astype(jnp.float32)
    choose = code[:, None] - 1.0 == jnp.arange(kept_factors, dtype=jnp.float32)[None, :]
    gather_places = jnp.dot(flat, down_factor, preferred_element_type=jnp.float32).reshape(
        count, kept_factors, rank_padding
    )
    gather_places = jnp.sum(gather_places * choose.astype(jnp.float32)[:, :, None], axis=1)
    gather_places = lax.psum(gather_places, "tensor")
    live_positions = (
        jnp.arange(rank_padding, dtype=jnp.float32)[None, :] < row_rank_value[:, None]
    ).astype(jnp.float32)
    narrow_input = (
        gather_places
        * live_positions
        * (adapter_strength / jnp.maximum(row_rank_value, 1.0))[:, None]
    ).astype(jnp.bfloat16)
    rank_spread = (narrow_input[:, None, :] * choose.astype(jnp.bfloat16)[:, :, None]).reshape(
        count, kept_factors * rank_padding
    )
    narrow_output = jnp.dot(rank_spread, up_factor, preferred_element_type=jnp.float32).astype(
        jnp.bfloat16
    )
    narrow_output = narrow_output.reshape(block.shape[0], block.shape[1], adapter_portion)
    returned = lax.all_to_all(narrow_output, "store", split_axis=0, concat_axis=0, tiled=True)
    low_home = lax.dot_general(
        packer,
        returned.reshape(stores * capacity, adapter_portion),
        (((0,), (0,)), ((), ())),
        preferred_element_type=jnp.float32,
    )
    partial_sum = jnp.dot(mixed, output_projection, preferred_element_type=jnp.float32)
    gain = output_norm_gain.astype(jnp.float32)
    stream_mine = lax.dynamic_slice_in_dim(stream_f, column * adapter_portion, adapter_portion, 1)
    piece = (
        lax.dynamic_slice_in_dim(partial_sum, column * adapter_portion, adapter_portion, 1)
        + low_home
    )
    summand = lax.dynamic_update_slice_in_dim(partial_sum, piece, column * adapter_portion, 1)
    projected = lax.psum(summand, "tensor")
    mean = jnp.mean(projected * projected, axis=-1, keepdims=True)
    mine = lax.dynamic_slice_in_dim(projected, column * adapter_portion, adapter_portion, 1)
    return (stream_mine + mine * lax.rsqrt(mean + epsilon) * gain).astype(jnp.bfloat16)


def solution(mesh):
    in_specs = (
        P(("groups", "store"), None),
        P(),
        P("tensor"),
        P(None, "tensor"),
        P(None, None, "tensor"),
        P("tensor", None),
        P(None, ("groups", "store"), "tensor", None, None),
        P(("groups", "store")),
        P(("groups", "store")),
        P("groups"),
        P("groups"),
        P("tensor", ("groups", "store"), None),
        P(("groups", "store"), None, "tensor"),
    )
    out_specs = P(("groups", "store"), "tensor")
    return jax.shard_map(
        per_device, mesh=mesh, in_specs=in_specs, out_specs=out_specs, check_vma=False
    )
```

profile of v0, /device:TPU:0, one launch (start us, length us, event | category | flops | bytes accessed | tf_op | source)
XLA Modules:
  0.0 190.6 jit_solution(8319756466328687001)
XLA Ops:
  6.5 0.0 copy-start
  6.5 0.9 select_reduce_fusion.1
  7.4 0.1 fusion.32
  7.5 0.2 reduce_window_sum.11
  7.7 0.2 select_reduce_fusion
  7.9 0.1 convolution_convert_fusion.1
  8.0 0.1 reshape.296
  8.1 0.6 copy.47
  8.8 6.3 %all-to-all-start = ((bf16[4,32,2]{1,2,0:T(2,128)(2,1)}), bf16[4,32,2]{1,2,0:T(2,128)(2,1)S(1)}, u32[]{:S(2)}, u32[]{:S(2)}) async-start(bf16[4,32,2]{1,2,0:T(2,128)(2,1)} %copy.47), calls=%async_computation | async-start | bytes 4096 | tf_op jit(solution)/shard_map/all_to_all | solution.py:125
  15.1 0.7 convert_element_type.129
  15.7 1.3 iota_compare_fusion.5
  17.1 0.7 convert_element_type.127
  17.8 1.6 multiply_reduce_fusion.1
  19.4 10.4 %copy.58 = bf16[576,8,2,512]{3,1,2,0:T(8,128)(2,1)} copy(bf16[576,8,2,512]{3,2,1,0:T(2,128)(2,1)} %bitcast.85) | data formatting | bytes 18874368
  29.8 0.0 copy-start.1
  29.8 12.8 %copy.40 = bf16[1024,4608]{1,0:T(8,128)(2,1)} copy(bf16[1024,4608]{0,1:T(8,128)(2,1)} %bitcast.84) | data formatting | bytes 18874368 | tf_op jit(solution)/shard_map/dot_general | solution.py:93
  42.6 0.0 copy-done.1
  42.6 5.3 %fusion.8 = f32[128,2,4,128]{0,3,2,1:T(8,128)S(1)} fusion(bf16[2,4,128,4608]{3,2,1,0:T(8,128)(2,1)} %bitcast.86, f32[4608]{0:T(1024)S(1)} %convert_element_type.127, f32[128]{0:T(128)S(1)} %add_rsqrt_fusion.1, bf16[128,4608]{1,0:T(8,128)(2,1)S(1)} %copy-done.1), kind=kOutput, calls=%fused_computation.15 | convolution fusion | flops 1210318848 | bytes 11160064 | tf_op jit(solution)/shard_map/dot_general | solution.py:93
  47.9 0.2 multiply_cosine_fusion
  48.1 0.1 copy.38
  48.2 0.1 copy.39
  48.4 0.1 copy.55
  48.6 5.1 %convolution_bitcast_fusion.1 = f32[16,8,8,128]{3,1,2,0:T(8,128)S(1)} fusion(bf16[4608,1024]{1,0:T(8,128)(2,1)} %param.16, f32[4608]{0:T(1024)S(1)} %convert_element_type.127, f32[128]{0:T(128)S(1)} %add_rsqrt_fusion.1, bf16[128,4608]{1,0:T(8,128)(2,1)S(1)} %copy-done.1), kind=kOutput, calls=%fused_computation.13 | convolution fusion | flops 1210318848 | bytes 11160064 | tf_op jit(solution)/shard_map/dot_general | solution.py:88
  53.7 0.1 copy.57
  53.8 0.3 subtract_convert_fusion
  54.1 0.0 copy-start.2
  54.1 0.7 copy-done.2
  54.8 1.5 multiply_reduce_fusion.2
  56.3 0.1 copy.54
  56.4 13.2 %fusion.49 = (f32[128,4,2]{2,1,0:T(4,128)S(1)}, f32[128,4,2,128]{3,2,1,0:T(2,128)}) fusion(bf16[2,128,4,128,128]{4,3,2,1,0:T(8,128)(2,1)} %param.19, bf16[128,4,2,64]{3,2,1,0:T(2,128)(2,1)} %bitcast.93, bf16[128,4,2,64]{3,2,1,0:T(2,128)(2,1)S(1)} %bitcast.91, pred[128,128]{1,0:T(8,128)(4,1)} %iota_compare_fusion.5), kind=kOutput, calls=%fused_computation.95 | convolution fusion | flops 34470912 | bytes 17715200 | tf_op jit(solution)/shard_map/bgrd,bgld->bgrl/dot_general | solution.py:39
  69.6 0.1 copy.41
  69.7 0.2 copy.42
  69.9 2.3 %fusion.24 = f32[128,4,2]{2,1,0:T(4,128)S(1)} fusion(f32[128,4,2,128]{3,2,1,0:T(2,128)} %get-tuple-element.20, f32[128,4,2]{2,1,0:T(4,128)S(1)} %copy.42), kind=kLoop, calls=%fused_computation.31 | loop fusion | flops 261120 | bytes 532480 | tf_op jit(solution)/shard_map/reduce_sum | solution.py:51
  72.3 0.1 copy.43
  72.4 0.2 copy.44
  72.6 0.2 copy.45
  72.8 0.8 copy.46
  73.6 8.2 %fusion.16 = bf16[128,4,2,128]{3,2,1,0:T(2,128)(2,1)S(1)} fusion(bf16[2,128,4,128,128]{4,3,2,1,0:T(8,128)(2,1)} %param.19, f32[128,4,2,128]{3,2,1,0:T(2,128)} %get-tuple-element.20, f32[128,4,128]{2,1,0:T(4,128)} %copy.46, f32[128,4,2]{2,1,0:T(4,128)S(1)} %copy.45, f32[128,4,2]{2,1,0:T(4,128)S(1)} %copy.44, f32[128,4,2]{2,1,0:T(4,128)S(1)} %copy.42), kind=kOutput, calls=%fused_computation.19 | convolution fusion | flops 34340864 | bytes 17838080 | tf_op jit(solution)/shard_map/bgrl,bgld->bgrd/dot_general | solution.py:54
  81.8 0.2 reshape.295
  82.0 0.9 convolution_convert_fusion
  82.9 0.0 all-to-all-done
  82.9 5.1 %all-to-all-start.1 = ((bf16[4,32,1024]{2,1,0:T(8,128)(2,1)}), bf16[4,32,1024]{2,1,0:T(8,128)(2,1)S(1)}, u32[]{:S(2)}, u32[]{:S(2)}) async-start(bf16[4,32,1024]{2,1,0:T(8,128)(2,1)} %bitcast.13), calls=%async_computation.1 | async-start | bytes 524288 | tf_op jit(solution)/shard_map/all_to_all | solution.py:124
  88.1 0.1 sub.54
  88.1 0.1 reshape.303
  88.3 8.1 %all-to-all-done.1 = bf16[4,32,1024]{2,1,0:T(8,128)(2,1)S(1)} async-done(((bf16[4,32,1024]{2,1,0:T(8,128)(2,1)}), bf16[4,32,1024]{2,1,0:T(8,128)(2,1)S(1)}, u32[]{:S(2)}, u32[]{:S(2)}) %all-to-all-start.1) | async-done | bytes 262176 | tf_op jit(solution)/shard_map/all_to_all | solution.py:124
  96.3 1.7 fusion.19
  98.0 10.3 %psum.14 = f32[128,64]{0,1:T(8,128)S(1)} all-reduce(f32[128,64]{0,1:T(8,128)S(1)} %fusion.19), channel_id=1, replica_groups=mesh['groups'=2,'store'=4,'tensor'=4] {'tensor'}, use_global_device_ids=true, to_apply=%region_8.9 | all-reduce | flops 8192 | bytes 65536 | tf_op jit(solution)/shard_map/psum | solution.py:135
  108.3 0.0 copy-done
  108.3 1.1 fusion.7
  109.4 3.5 %all-to-all-start.2 = ((bf16[4,32,1152]{2,1,0:T(8,128)(2,1)}), bf16[4,32,1152]{2,1,0:T(8,128)(2,1)S(1)}, u32[]{:S(2)}, u32[]{:S(2)}) async-start(bf16[4,32,1152]{2,1,0:T(8,128)(2,1)} %bitcast.20), calls=%async_computation.2 | async-start | bytes 589824 | tf_op jit(solution)/shard_map/all_to_all | solution.py:151
  112.9 0.0 all-reduce.2.cloned.1.call-start
  112.9 6.5 %fusion.50 = f32[128,4608]{1,0:T(8,128)} fusion(bf16[128,1024]{1,0:T(8,128)(2,1)S(1)} %reshape.295, bf16[1024,4608]{1,0:T(8,128)(2,1)} %param.18), kind=kOutput, calls=%fused_computation.96 | convolution fusion | flops 1207959552 | bytes 12058624 | tf_op jit(solution)/shard_map/dot_general | solution.py:158
  119.5 3.5 %all-to-all-done.2 = bf16[4,32,1152]{2,1,0:T(8,128)(2,1)S(1)} async-done(((bf16[4,32,1152]{2,1,0:T(8,128)(2,1)}), bf16[4,32,1152]{2,1,0:T(8,128)(2,1)S(1)}, u32[]{:S(2)}, u32[]{:S(2)}) %all-to-all-start.2) | async-done | bytes 294944 | tf_op jit(solution)/shard_map/all_to_all | solution.py:151
  123.0 2.2 %fusion.6 = f32[128,4608]{1,0:T(8,128)} fusion(f32[128,4608]{1,0:T(8,128)} %fusion.50, s32[]{:T(128)S(6)} %select_n.38, bf16[128,1152]{1,0:T(8,128)(2,1)S(1)} %bitcast.88, s32[128]{0:T(128)S(1)} %multiply_add_fusion), kind=kOutput, calls=%fused_computation.7 | convolution fusion | flops 37912576 | bytes 1475076 | tf_op jit(solution)/shard_map/dot_general | solution.py:152
  125.2 0.0 copy-start.3
  125.2 0.0 all-reduce.2.cloned.1.call-update
  125.2 1.6 convert_element_type.126
  126.8 0.0 copy-done.3
  126.8 52.9 %all-reduce.2.cloned.1.call-done = f32[128,4608]{1,0:T(8,128)} async-done(((f32[128,4608]{1,0:T(8,128)}), f32[128,4608]{1,0:T(8,128)}) %all-reduce.2.cloned.1.call-update) | async-done | bytes 2359312 | tf_op jit(solution)/shard_map/psum | solution.py:166
  179.7 1.9 %multiply_reduce_fusion = f32[128]{0:T(128)S(1)} fusion(f32[128,4608]{1,0:T(8,128)} %all-reduce.2.cloned.1.call-done), kind=kLoop, calls=%fused_computation.10 | loop fusion | flops 1179520 | bytes 2359808 | tf_op jit(solution)/shard_map/reduce_sum | solution.py:167
  181.6 2.1 %add_convert_fusion = bf16[128,1152]{1,0:T(8,128)(2,1)} fusion(f32[128,4608]{1,0:T(8,128)} %all-reduce.2.cloned.1.call-done, s32[]{:T(128)S(6)} %select_n.38, f32[128,4608]{1,0:T(8,128)} %convert_element_type.126, f32[1152]{0:T(1024)S(1)} %convert_element_type.149, f32[128]{0:T(128)S(1)} %add_rsqrt_fusion), kind=kLoop, calls=%fused_computation.25 | loop fusion | flops 589824 | bytes 1479684 | tf_op jit(solution)/shard_map/convert_element_type | solution.py:169
  (18 shorter events, 0.3 us)
Async XLA Ops:
  6.5 101.8 %copy-start = (bf16[8,64,1152]{2,1,0:T(8,128)(2,1)S(1)}, bf16[8,64,1152]{2,1,0:T(8,128)(2,1)}, u32[]{:S(2)}) copy-start(bf16[8,64,1152]{2,1,0:T(8,128)(2,1)} %param.25) | copy-start | bytes 3538948
  8.8 74.2 %all-to-all-start = ((bf16[4,32,2]{1,2,0:T(2,128)(2,1)}), bf16[4,32,2]{1,2,0:T(2,128)(2,1)S(1)}, u32[]{:S(2)}, u32[]{:S(2)}) async-start(bf16[4,32,2]{1,2,0:T(2,128)(2,1)} %copy.47), calls=%async_computation | async-start | bytes 4096 | tf_op jit(solution)/shard_map/all_to_all | solution.py:125
  29.8 12.8 %copy-start.1 = (bf16[128,4608]{1,0:T(8,128)(2,1)S(1)}, bf16[128,4608]{1,0:T(8,128)(2,1)}, u32[]{:S(2)}) copy-start(bf16[128,4608]{1,0:T(8,128)(2,1)} %param.13) | copy-start | bytes 3538948
  54.1 0.7 copy-start.2
  82.9 13.4 %all-to-all-start.1 = ((bf16[4,32,1024]{2,1,0:T(8,128)(2,1)}), bf16[4,32,1024]{2,1,0:T(8,128)(2,1)S(1)}, u32[]{:S(2)}, u32[]{:S(2)}) async-start(bf16[4,32,1024]{2,1,0:T(8,128)(2,1)} %bitcast.13), calls=%async_computation.1 | async-start | bytes 524288 | tf_op jit(solution)/shard_map/all_to_all | solution.py:124
  109.4 13.5 %all-to-all-start.2 = ((bf16[4,32,1152]{2,1,0:T(8,128)(2,1)}), bf16[4,32,1152]{2,1,0:T(8,128)(2,1)S(1)}, u32[]{:S(2)}, u32[]{:S(2)}) async-start(bf16[4,32,1152]{2,1,0:T(8,128)(2,1)} %bitcast.20), calls=%async_computation.2 | async-start | bytes 589824 | tf_op jit(solution)/shard_map/all_to_all | solution.py:151
  112.9 66.8 %all-reduce.2.cloned.1.call-start = ((), (), s32[]{:S(2)}) async-start(), calls=%async_computation.3 | async-start | bytes 4718592 | tf_op jit(solution)/shard_map/psum | solution.py:166
  125.2 1.7 copy-start.3
Sparse Core Ops, SparseCore 0:
  125.3 54.3 all-reduce.1
where the time goes:
time: 192 us; the launch traced here: 191 us
  waiting for transfers between devices  64.5 us (34%)
  matrix products  44.4 us (23%)
  local copies, waits for them, and re-layouts  27.1 us (14%)
  other arithmetic  15.7 us (8%)
  starting transfers between devices  14.9 us (8%)
  between operations  13.6 us (7%)
  blocking collectives  10.3 us (5%)
    psum x1, waiting for transfers between devices, per_device(): projected = lax.psum(summand, 'tensor')  52.9 us
    dot_general x1, matrix products, attend(): jnp.einsum('bgrd,bgld->bgrl', query, keys, preferred_element_type=jnp.flo...  13.2 us
    dot_general x1, local copies, waits for them, and re-layouts, per_device(): jnp.dot(normed, key_value_weight.reshape(width, -1), preferred_element_ty...  12.8 us
    unnamed x11, local copies, waits for them, and re-layouts  11.4 us
    psum x1, blocking collectives, per_device(): gather_places = lax.psum(gather_places, 'tensor')  10.3 us
    dot_general x1, matrix products, attend(): jnp.einsum('bgrl,bgld->bgrd', probs, values, preferred_element_type=jnp.f...  8.23 us
    all_to_all x1, waiting for transfers between devices, per_device(): lax.all_to_all(outgoing, 'store', split_axis=0, concat_axis=0, tiled=True)  8.09 us
    dot_general x1, matrix products, per_device(): jnp.dot(mixed, output_projection, preferred_element_type=jnp.float32)  6.54 us
  transfers between devices with their start and end apart: 4, of which 3 were waited for; matrix products, arithmetic and copies ran while one was open for 40% of the time, Pallas kernels for 0%

commit v1 on v0

--- a/solution.py
+++ b/solution.py
@@ -1,9 +1,14 @@
+import functools
 import math
 
 import jax
 import jax.numpy as jnp
 from jax import lax
+from jax.experimental import pallas as pl
+from jax.experimental.pallas import tpu as pltpu
 from jax.sharding import PartitionSpec as P
+
+MESH = pl.DeviceIdType.MESH
 
 HEAD_WIDTH = 128
 
@@ -57,6 +62,324 @@
         + own_prob.astype(jnp.float32)[..., None] * value_new.astype(jnp.float32)[:, :, None, :]
     )
     return mixed.astype(jnp.bfloat16).reshape(query.shape[0], -1)
+
+
+NT = (((1,), (1,)), ((), ()))
+TN = (((0,), (0,)), ((), ()))
+
+
+def exchange_kernel(
+    stores,
+    column_count,
+    kept,
+    capacity,
+    mixed_ref,
+    index_ref,
+    slot_ref,
+    rank_ref,
+    down_ref,
+    up_ref,
+    gain_ref,
+    stream_ref,
+    weight_ref,
+    out_ref,
+    weight_buf,
+    stream_buf,
+    out_buf,
+    in_buf,
+    part_buf,
+    part_in,
+    cross_buf,
+    cross_in,
+    low_buf,
+    low_in,
+    back_buf,
+    back_in,
+    stat_buf,
+    stat_in,
+    load_sem,
+    row_send,
+    row_recv,
+    part_send,
+    part_recv,
+    low_send,
+    low_recv,
+    back_send,
+    back_recv,
+    stat_send,
+    stat_recv,
+):
+    rows, depth = mixed_ref.shape
+    portion = gain_ref.shape[1]
+    rank_width = down_ref.shape[0] // kept
+    width = portion * column_count
+    f32 = jnp.float32
+    bf16 = jnp.bfloat16
+    store = lax.axis_index("store")
+    column = lax.axis_index("tensor")
+    chip = column // 2
+    core = column % 2
+    chunks = [(1 - chip) * 2 + 1 - core, chip * 2 + 1 - core, (1 - chip) * 2 + core, column]
+    partner = chip * 2 + 1 - core
+    across = (1 - chip) * 2 + core
+
+    loads = []
+    for i, chunk in enumerate(chunks):
+        start = pl.multiple_of(chunk * portion, 128)
+        loads.append(
+            pltpu.make_async_copy(
+                weight_ref.at[:, pl.ds(start, portion)], weight_buf.at[i], load_sem.at[i]
+            )
+        )
+    mine = pl.multiple_of(column * portion, 128)
+    loads.append(
+        pltpu.make_async_copy(
+            stream_ref.at[:, pl.ds(mine, portion)], stream_buf, load_sem.at[column_count]
+        )
+    )
+    for load in loads:
+        load.start()
+
+    barrier = pltpu.get_barrier_semaphore()
+    for k in range(1, stores):
+        pl.semaphore_signal(
+            barrier, inc=1, device_id={"store": (store + k) % stores}, device_id_type=MESH
+        )
+    for k in range(1, column_count):
+        pl.semaphore_signal(
+            barrier, inc=1, device_id={"tensor": (column + k) % column_count}, device_id_type=MESH
+        )
+
+    adapters = slot_ref.shape[1]
+    match = (
+        lax.broadcasted_iota(jnp.int32, (adapters, rows), 0) == index_ref[...]
+    ).astype(f32)
+    slot = jnp.dot(
+        jnp.broadcast_to(slot_ref[...].astype(f32), (8, adapters)), match, preferred_element_type=f32
+    )
+    rank = jnp.dot(
+        jnp.broadcast_to(rank_ref[...].astype(f32), (8, adapters)), match, preferred_element_type=f32
+    )
+    owner = jnp.zeros((8, rows), f32)
+    for s in range(1, stores):
+        owner = owner + (slot >= float(s * kept)).astype(f32)
+    within = slot - owner * float(kept)
+    turned = owner - store.astype(f32)
+    turned = jnp.where(turned < 0.0, turned + float(stores), turned)
+    target = (lax.broadcasted_iota(jnp.int32, (8, rows), 0).astype(f32) == turned).astype(f32)
+    earlier = (
+        lax.broadcasted_iota(jnp.int32, (rows, rows), 0)
+        < lax.broadcasted_iota(jnp.int32, (rows, rows), 1)
+    ).astype(f32)
+    before = jnp.dot(target, earlier, preferred_element_type=f32)
+    place = jnp.sum(before * target, axis=0, keepdims=True) + turned[0:1] * float(capacity)
+    packer_f = (
+        lax.broadcasted_iota(jnp.int32, (stores * capacity, rows), 0).astype(f32) == place
+    ).astype(f32)
+    packer = packer_f.astype(bf16)
+    line = lax.broadcasted_iota(jnp.int32, (128, rows), 0)
+    labels = jnp.where(line == 0, within[0:1] + 1.0, jnp.where(line == 1, rank[0:1], 0.0))
+    labels = lax.dot_general(packer, labels.astype(bf16), NT, preferred_element_type=f32)
+    mixed = mixed_ref[...]
+    outgoing = jnp.dot(packer, mixed, preferred_element_type=f32)
+    out_buf[:, :, 0:depth] = outgoing.astype(bf16).reshape(stores, capacity, depth)
+    out_buf[:, :, depth : depth + 128] = labels.astype(bf16).reshape(stores, capacity, 128)
+
+    pl.semaphore_wait(barrier, stores + column_count - 2)
+
+    def row_copy(k):
+        return pltpu.make_async_remote_copy(
+            src_ref=out_buf.at[k],
+            dst_ref=in_buf.at[k - 1],
+            send_sem=row_send.at[k - 1],
+            recv_sem=row_recv.at[k - 1],
+            device_id={"store": (store + k) % stores},
+            device_id_type=MESH,
+        )
+
+    row_copies = [row_copy(k) for k in range(1, stores)]
+    for copy in row_copies:
+        copy.start()
+
+    part_copies = []
+    for i in range(2):
+        loads[i].wait()
+        part_buf[i] = jnp.dot(mixed, weight_buf[i], preferred_element_type=f32).astype(bf16)
+        copy = pltpu.make_async_remote_copy(
+            src_ref=part_buf.at[i],
+            dst_ref=part_in.at[i],
+            send_sem=part_send.at[i],
+            recv_sem=part_recv.at[i],
+            device_id={"tensor": partner},
+            device_id_type=MESH,
+        )
+        copy.start()
+        part_copies.append(copy)
+    loads[2].wait()
+    crossing = jnp.dot(mixed, weight_buf[2], preferred_element_type=f32)
+    part_copies[0].wait()
+    cross_buf[...] = (crossing + part_in[0].astype(f32)).astype(bf16)
+    cross_copy = pltpu.make_async_remote_copy(
+        src_ref=cross_buf,
+        dst_ref=cross_in,
+        send_sem=part_send.at[2],
+        recv_sem=part_recv.at[2],
+        device_id={"tensor": across},
+        device_id_type=MESH,
+    )
+    cross_copy.start()
+
+    for copy in row_copies:
+        copy.wait()
+    block = jnp.concatenate([out_buf[0]] + [in_buf[k] for k in range(stores - 1)], axis=0)
+    code = block[:, depth : depth + 1].astype(f32)
+    row_rank = block[:, depth + 1 : depth + 2].astype(f32)
+    full = lax.dot_general(block[:, 0:depth], down_ref[...], NT, preferred_element_type=f32)
+    count = stores * capacity
+    lane = lax.broadcasted_iota(jnp.int32, (count, kept * rank_width), 1).astype(f32)
+    choose = jnp.logical_and(
+        lane >= (code - 1.0) * float(rank_width), lane < code * float(rank_width)
+    )
+    full = jnp.where(choose, full, 0.0)
+    coordinates = full[:, 0:128]
+    for i in range(1, kept * rank_width // 128):
+        coordinates = coordinates + full[:, i * 128 : (i + 1) * 128]
+    low_buf[...] = coordinates.astype(bf16)
+    low_copies = []
+    for k in range(1, column_count):
+        copy = pltpu.make_async_remote_copy(
+            src_ref=low_buf,
+            dst_ref=low_in.at[k - 1],
+            send_sem=low_send.at[k - 1],
+            recv_sem=low_recv.at[k - 1],
+            device_id={"tensor": (column + k) % column_count},
+            device_id_type=MESH,
+        )
+        copy.start()
+        low_copies.append(copy)
+
+    loads[3].wait()
+    own = jnp.dot(mixed, weight_buf[3], preferred_element_type=f32)
+    part_copies[1].wait()
+    own = own + part_in[1].astype(f32)
+
+    for k in range(column_count - 1):
+        low_copies[k].wait()
+        coordinates = coordinates + low_in[k].astype(f32)
+    place_in_rank = lax.broadcasted_iota(jnp.int32, (count, 128), 1) % rank_width
+    live = place_in_rank.astype(f32) < row_rank
+    narrow = jnp.where(live, coordinates * (adapter_strength / jnp.maximum(row_rank, 1.0)), 0.0)
+    spread = jnp.concatenate([narrow] * (kept * rank_width // 128), axis=1)
+    spread = jnp.where(choose, spread, 0.0).astype(bf16)
+    wide = jnp.dot(spread, up_ref[...], preferred_element_type=f32).astype(bf16)
+    back_buf[...] = wide.reshape(stores, capacity, portion)
+    back_copies = []
+    for k in range(1, stores):
+        copy = pltpu.make_async_remote_copy(
+            src_ref=back_buf.at[k],
+            dst_ref=back_in.at[k - 1],
+            send_sem=back_send.at[k - 1],
+            recv_sem=back_recv.at[k - 1],
+            device_id={"store": (store + stores - k) % stores},
+            device_id_type=MESH,
+        )
+        copy.start()
+        back_copies.append(copy)
+
+    unpacker = packer_f.T.astype(bf16)
+    cross_copy.wait()
+    own = own + cross_in[...].astype(f32)
+    for copy in back_copies:
+        copy.wait()
+    returned = jnp.concatenate([back_buf[0]] + [back_in[k] for k in range(stores - 1)], axis=0)
+    projected = own + jnp.dot(unpacker, returned, preferred_element_type=f32)
+
+    squares = jnp.sum(projected * projected, axis=1, keepdims=True)
+    stat_buf[...] = jnp.broadcast_to(squares, (rows, 128)).T[0:8]
+    stat_copies = []
+    for k in range(1, column_count):
+        copy = pltpu.make_async_remote_copy(
+            src_ref=stat_buf,
+            dst_ref=stat_in.at[k - 1],
+            send_sem=stat_send.at[k - 1],
+            recv_sem=stat_recv.at[k - 1],
+            device_id={"tensor": (column + k) % column_count},
+            device_id_type=MESH,
+        )
+        copy.start()
+        stat_copies.append(copy)
+    loads[4].wait()
+    total = stat_buf[0:1]
+    for k in range(column_count - 1):
+        stat_copies[k].wait()
+        total = total + stat_in[k, 0:1]
+    total = jnp.broadcast_to(total, (128, rows)).T[:, 0:1]
+    factor = lax.rsqrt(total * (1.0 / width) + epsilon)
+    out_ref[...] = (
+        stream_buf[...].astype(f32) + projected * factor * gain_ref[...].astype(f32)
+    ).astype(bf16)
+
+
+def exchange(mixed, index, slots, ranks, down, up, gain, stream, weight):
+    stores = lax.axis_size("store")
+    column_count = lax.axis_size("tensor")
+    rows, depth = mixed.shape
+    kept = down.shape[1]
+    rank_width = down.shape[2]
+    portion = up.shape[2]
+    capacity = rows // 4
+    down = jnp.transpose(down, (1, 2, 0)).reshape(kept * rank_width, depth)
+    up = up.reshape(kept * rank_width, portion)
+    bf16 = jnp.bfloat16
+    dma = pltpu.SemaphoreType.DMA
+    vmem = pl.BlockSpec(memory_space=pltpu.VMEM)
+    hbm = pl.BlockSpec(memory_space=pl.ANY)
+    return pl.pallas_call(
+        functools.partial(exchange_kernel, stores, column_count, kept, capacity),
+        out_shape=jax.ShapeDtypeStruct((rows, portion), bf16),
+        in_specs=[vmem] * 7 + [hbm] * 2,
+        out_specs=vmem,
+        scratch_shapes=[
+            pltpu.VMEM((column_count, depth, portion), bf16),
+            pltpu.VMEM((rows, portion), bf16),
+            pltpu.VMEM((stores, capacity, depth + 128), bf16),
+            pltpu.VMEM((stores - 1, capacity, depth + 128), bf16),
+            pltpu.VMEM((2, rows, portion), bf16),
+            pltpu.VMEM((2, rows, portion), bf16),
+            pltpu.VMEM((rows, portion), bf16),
+            pltpu.VMEM((rows, portion), bf16),
+            pltpu.VMEM((stores * capacity, 128), bf16),
+            pltpu.VMEM((column_count - 1, stores * capacity, 128), bf16),
+            pltpu.VMEM((stores, capacity, portion), bf16),
+            pltpu.VMEM((stores - 1, capacity, portion), bf16),
+            pltpu.VMEM((8, rows), jnp.float32),
+            pltpu.VMEM((column_count - 1, 8, rows), jnp.float32),
+            dma((column_count + 1,)),
+            dma((stores - 1,)),
+            dma((stores - 1,)),
+            dma((3,)),
+            dma((3,)),
+            dma((column_count - 1,)),
+            dma((column_count - 1,)),
+            dma((stores - 1,)),
+            dma((stores - 1,)),
+            dma((column_count - 1,)),
+            dma((column_count - 1,)),
+        ],
+        compiler_params=pltpu.CompilerParams(
+            collective_id=0, has_side_effects=True, vmem_limit_bytes=40 << 20
+        ),
+    )(
+        mixed,
+        index.reshape(1, -1),
+        slots.reshape(1, -1),
+        ranks.reshape(1, -1),
+        down,
+        up,
+        gain.reshape(1, -1),
+        stream,
+        weight,
+    )
 
 
 def per_device(
@@ -97,6 +420,18 @@
     mixed = attend(
         query, key_new, value_new, cached_key_value[0], cached_key_value[1], row_cache_length
     )
+    if lax.axis_size("tensor") == 4 and adapter_portion % 128 == 0 and row_count == 128:
+        return exchange(
+            mixed,
+            row_adapter_index,
+            adapter_slot_table,
+            adapter_rank_table,
+            adapter_down_weight,
+            adapter_up_weight,
+            output_norm_gain,
+            stream,
+            output_projection,
+        )
     adapters = adapter_slot_table.shape[0]
     match = row_adapter_index[:, None] == jnp.arange(adapters)[None, :]
     slot = jnp.sum(jnp.where(match, adapter_slot_table[None, :], 0), axis=1)

time: 192 us -> 103 us (0.54)
  waiting for transfers between devices: 64.5 us -> 0 us
  Pallas kernels: 0 us -> 29.7 us
  starting transfers between devices: 14.9 us -> 0 us
  between operations: 13.6 us -> 0.26 us
  matrix products: 44.4 us -> 32.2 us
  blocking collectives: 10.3 us -> 0 us
  other arithmetic: 15.7 us -> 5.87 us
  local copies, waits for them, and re-layouts: 27.1 us -> 34 us
    psum x1 -> x0, waiting for transfers between devices: 52.9 us -> none  [per_device(): projected = lax.psum(summand, 'tensor')]
    pallas_call x0 -> x1, Pallas kernels: none -> 29.7 us  [exchange(): pl.pallas_call(functools.partial(exchange_kernel, stores, column_count, k...]
    all_to_all x3 -> x0, starting transfers between devices: 14.9 us -> none  [the longest x1 6.32 us: per_device(): lax.all_to_all(labels, 'store', split_axis=0, concat_axis=0, tiled=True)]
    dot_general x6 -> x0, matrix products: 12.6 us -> none  [the longest x1 6.54 us: per_device(): jnp.dot(mixed, output_projection, preferred_element_type=jnp.float32)]
    all_to_all x3 -> x0, waiting for transfers between devices: 11.6 us -> none  [the longest x1 8.09 us: per_device(): lax.all_to_all(outgoing, 'store', split_axis=0, concat_axis=0, tiled=True)]
    psum x1 -> x0, blocking collectives: 10.3 us -> none  [per_device(): gather_places = lax.psum(gather_places, 'tensor')]
    unnamed x11 -> x28, local copies, waits for them, and re-layouts: 11.4 us -> 16 us
    convert_element_type x9 -> x0, other arithmetic: 3.88 us -> none  [the longest x1 2.1 us: per_device(): (stream_mine + mine * lax.rsqrt(mean + epsilon) * gain).astype(jnp.bfloat16)]
  transfers between devices with their start and end apart: 4 -> 0, of which waited for: 3 -> 0; matrix products, arithmetic and copies ran while one was open for 40% -> 0% of each run, Pallas kernels for 0% -> 0%
where the time goes in v1:
time: 103 us; the launch traced here: 102 us
  local copies, waits for them, and re-layouts  34 us (33%)
  matrix products  32.2 us (31%)
  Pallas kernels  29.7 us (29%)
  other arithmetic  5.87 us (6%)
    pallas_call x1, Pallas kernels, exchange(): pl.pallas_call(functools.partial(exchange_kernel, stores, column_count, k...  29.7 us
    unnamed x28, local copies, waits for them, and re-layouts  16 us
    dot_general x1, local copies, waits for them, and re-layouts, per_device(): jnp.dot(normed, key_value_weight.reshape(width, -1), preferred_element_ty...  12.9 us
    dot_general x1, matrix products, attend(): jnp.einsum('bgrd,bgld->bgrl', query, keys, preferred_element_type=jnp.flo...  12.6 us
    dot_general x1, matrix products, attend(): jnp.einsum('bgrl,bgld->bgrd', probs, values, preferred_element_type=jnp.f...  9.27 us
    dot_general x1, matrix products, per_device(): jnp.dot(normed, key_value_weight.reshape(width, -1), preferred_element_ty...  5.27 us
    dot_general x1, matrix products, per_device(): jnp.dot(normed, query_projection, preferred_element_type=jnp.float32)  5.11 us

profile of v1, /device:TPU:0, one launch (start us, length us, event | category | flops | bytes accessed | tf_op | source)
XLA Modules:
  0.0 102.0 jit_solution(12459946466155652042)
XLA Ops:
  0.0 0.7 convert_element_type.45
  0.7 1.6 %fusion.6 = f32[128]{0:T(128)S(1)} fusion(bf16[128,4608]{1,0:T(8,128)(2,1)} %stream_ref.1), kind=kLoop, calls=%fused_computation.8 | loop fusion | flops 1769344 | bytes 1180160 | tf_op jit(solution)/shard_map/reduce_sum | solution.py:23
  2.3 10.4 %copy.44 = bf16[576,8,2,512]{3,1,2,0:T(8,128)(2,1)} copy(bf16[576,8,2,512]{3,2,1,0:T(2,128)(2,1)} %bitcast.55) | data formatting | bytes 18874368
  12.7 0.0 copy-start
  12.7 12.9 %copy.27 = bf16[1024,4608]{1,0:T(8,128)(2,1)} copy(bf16[1024,4608]{0,1:T(8,128)(2,1)} %bitcast.54) | data formatting | bytes 18874368 | tf_op jit(solution)/shard_map/dot_general | solution.py:416
  25.6 0.0 copy-done
  25.6 0.0 copy-start.11
  25.6 5.3 %fusion.9 = f32[128,2,4,128]{0,3,2,1:T(8,128)S(1)} fusion(bf16[2,4,128,4608]{3,2,1,0:T(8,128)(2,1)} %bitcast.56, bf16[128,4608]{1,0:T(8,128)(2,1)S(1)} %copy-done, f32[4608]{0:T(1024)S(1)} %convert_element_type.45, f32[128]{0:T(128)S(1)} %add_rsqrt_fusion), kind=kOutput, calls=%fused_computation.12 | convolution fusion | flops 1210318848 | bytes 11160064 | tf_op jit(solution)/shard_map/dot_general | solution.py:416
  30.9 0.0 copy-done.11
  30.9 0.2 multiply_cosine_fusion
  31.2 0.1 copy.41
  31.3 5.1 %convolution_bitcast_fusion = f32[16,8,8,128]{3,1,2,0:T(8,128)S(1)} fusion(bf16[4608,1024]{1,0:T(8,128)(2,1)} %param.16, bf16[128,4608]{1,0:T(8,128)(2,1)S(1)} %copy-done, f32[4608]{0:T(1024)S(1)} %convert_element_type.45, f32[128]{0:T(128)S(1)} %add_rsqrt_fusion), kind=kOutput, calls=%fused_computation.11 | convolution fusion | flops 1210318848 | bytes 11160064 | tf_op jit(solution)/shard_map/dot_general | solution.py:411
  36.5 0.1 copy.43
  36.6 0.1 copy.25
  36.7 0.1 copy.26
  36.8 0.3 subtract_convert_fusion
  37.0 1.5 %multiply_reduce_fusion = f32[128,4,2]{2,1,0:T(4,128)S(1)} fusion(f32[128,4,128]{2,1,0:T(4,128)S(1)} %copy.41, bf16[128,4,2,64]{3,2,1,0:T(2,128)(2,1)S(1)} %bitcast.60, bf16[128,4,2,64]{3,2,1,0:T(2,128)(2,1)S(1)} %bitcast.58), kind=kLoop, calls=%fused_computation.18 | loop fusion | flops 916480 | bytes 528384
  38.5 0.1 copy.40
  38.6 0.1 iota_compare_fusion
  38.8 12.6 %fusion.32 = (f32[128,4,2]{2,1,0:T(4,128)S(1)}, f32[128,4,2,128]{3,2,1,0:T(2,128)S(1)}) fusion(bf16[2,128,4,128,128]{4,3,2,1,0:T(8,128)(2,1)} %param.19, bf16[128,4,2,64]{3,2,1,0:T(2,128)(2,1)S(1)} %bitcast.61, bf16[128,4,2,64]{3,2,1,0:T(2,128)(2,1)S(1)} %bitcast.59, pred[128,128]{1,0:T(8,128)(4,1)S(1)} %iota_compare_fusion), kind=kOutput, calls=%fused_computation.44 | convolution fusion | flops 34470912 | bytes 17584128 | tf_op jit(solution)/shard_map/bgrd,bgld->bgrl/dot_general | solution.py:44
  51.4 0.0 copy-start.9
  51.4 0.1 copy.28
  51.5 0.2 copy.29
  51.7 0.0 copy-start.8
  51.7 1.4 %fusion.25 = f32[128,4,2]{2,1,0:T(4,128)S(1)} fusion(f32[128,4,2,128]{3,2,1,0:T(2,128)S(1)} %get-tuple-element.14, f32[128,4,2]{2,1,0:T(4,128)S(1)} %copy.29), kind=kLoop, calls=%fused_computation.23 | loop fusion | flops 261120 | bytes 532480 | tf_op jit(solution)/shard_map/reduce_sum | solution.py:56
  53.1 0.1 copy.30
  53.2 0.9 copy.31
  54.1 0.0 copy-done.8
  54.1 0.8 copy.32
  54.9 0.0 copy-done.9
  55.0 0.8 copy.33
  55.8 0.0 copy-start.10
  55.8 0.0 copy-start.2
  55.8 0.0 copy-start.3
  55.8 0.0 copy-start.5
  55.8 0.0 copy-start.6
  55.8 0.0 copy-start.7
  55.8 9.3 %fusion.17 = bf16[128,4,2,128]{3,2,1,0:T(2,128)(2,1)} fusion(bf16[2,128,4,128,128]{4,3,2,1,0:T(8,128)(2,1)} %param.19, f32[128,4,2,128]{3,2,1,0:T(2,128)} %copy-done.9, f32[128,4,128]{2,1,0:T(4,128)} %copy.33, f32[128,4,2]{2,1,0:T(4,128)} %copy.32, f32[128,4,2]{2,1,0:T(4,128)} %copy.31, f32[128,4,2]{2,1,0:T(4,128)} %copy-done.8), kind=kOutput, calls=%fused_computation.16 | convolution fusion | flops 34340864 | bytes 18612224 | tf_op jit(solution)/shard_map/bgrl,bgld->bgrd/dot_general | solution.py:59
  65.1 1.8 %reshape.124.mixed_ref = bf16[128,1024]{1,0:T(8,128)(2,1)} reshape(bf16[128,4,2,128]{3,2,1,0:T(2,128)(2,1)} %fusion.17) | data formatting | bytes 524288 | tf_op jit(solution)/shard_map/reshape | solution.py:64
  66.9 0.0 copy-done.10
  66.9 0.0 copy-done.2
  66.9 0.0 copy-done.3
  66.9 0.0 copy-done.5
  66.9 0.0 copy-done.6
  67.0 0.0 copy-done.7
  67.0 0.0 copy-start.1
  67.0 3.7 %copy-done.1 = bf16[1024,4608]{1,0:T(8,128)(2,1)S(1)} copy-done((bf16[1024,4608]{1,0:T(8,128)(2,1)S(1)}, bf16[1024,4608]{1,0:T(8,128)(2,1)}, u32[]{:S(2)}) %copy-start.1) | copy-done | bytes 9437208
  70.7 0.0 copy-start.4
  70.7 0.9 copy-done.4
  71.6 29.7 %shard_map.127 = bf16[128,1152]{1,0:T(8,128)(2,1)S(1)} custom-call(bf16[128,1024]{1,0:T(8,128)(2,1)S(1)} %copy-done.4, s32[1,128]{1,0:T(1,128)S(1)} %bitcast.51, s32[1,32]{1,0:T(1,128)S(1)} %bitcast.52, s32[1,32]{1,0:T(1,128)S(1)} %bitcast.53, bf16[512,1024]{1,0:T(8,128)(2,1)S(1)} %bitcast.50, bf16[512,1152]{1,0:T(8,128)(2,1)S(1)} %bitcast.49, ...), custom_call_target="tpu_custom_call" | custom-call | tf_op jit(solution)/shard_map/pallas_call | solution.py:337
  101.3 0.7 copy.46
  (10 shorter events, 0.2 us)
Async XLA Ops:
  12.7 12.9 %copy-start = (bf16[128,4608]{1,0:T(8,128)(2,1)S(1)}, bf16[128,4608]{1,0:T(8,128)(2,1)}, u32[]{:S(2)}) copy-start(bf16[128,4608]{1,0:T(8,128)(2,1)} %stream_ref.1) | copy-start | bytes 3538948
  25.6 5.3 %copy-start.11 = (s32[128]{0:T(128)S(1)}, s32[128]{0:T(128)}, u32[]{:S(2)}) copy-start(s32[128]{0:T(128)} %param.20) | copy-start | bytes 1540
  51.4 3.6 %copy-start.9 = (f32[128,4,2,128]{3,2,1,0:T(2,128)}, f32[128,4,2,128]{3,2,1,0:T(2,128)S(1)}, u32[]{:S(2)}) copy-start(f32[128,4,2,128]{3,2,1,0:T(2,128)S(1)} %get-tuple-element.14) | copy-start | bytes 1572868
  51.7 2.4 %copy-start.8 = (f32[128,4,2]{2,1,0:T(4,128)}, f32[128,4,2]{2,1,0:T(4,128)S(1)}, u32[]{:S(2)}) copy-start(f32[128,4,2]{2,1,0:T(4,128)S(1)} %copy.29) | copy-start | bytes 12292
  55.8 11.1 %copy-start.10 = (bf16[1152]{0:T(1024)(128)(2,1)S(1)}, bf16[1152]{0:T(1024)(128)(2,1)}, u32[]{:S(2)}) copy-start(bf16[1152]{0:T(1024)(128)(2,1)} %param.15) | copy-start | bytes 6916
  55.8 11.1 %copy-start.2 = (bf16[8,64,1152]{2,1,0:T(8,128)(2,1)S(1)}, bf16[8,64,1152]{2,1,0:T(8,128)(2,1)}, u32[]{:S(2)}) copy-start(bf16[8,64,1152]{2,1,0:T(8,128)(2,1)} %param.25) | copy-start | bytes 3538948
  55.8 11.1 %copy-start.3 = (bf16[1024,8,64]{0,2,1:T(8,128)(2,1)S(1)}, bf16[1024,8,64]{0,2,1:T(8,128)(2,1)}, u32[]{:S(2)}) copy-start(bf16[1024,8,64]{0,2,1:T(8,128)(2,1)} %param.24) | copy-start | bytes 3145732
  55.8 11.1 %copy-start.5 = (s32[128]{0:T(128)S(1)}, s32[128]{0:T(128)}, u32[]{:S(2)}) copy-start(s32[128]{0:T(128)} %param.21) | copy-start | bytes 1540
  55.8 11.2 %copy-start.6 = (s32[32]{0:T(128)S(1)}, s32[32]{0:T(128)}, u32[]{:S(2)}) copy-start(s32[32]{0:T(128)} %param.22) | copy-start | bytes 388
  55.8 11.2 %copy-start.7 = (s32[32]{0:T(128)S(1)}, s32[32]{0:T(128)}, u32[]{:S(2)}) copy-start(s32[32]{0:T(128)} %param.23) | copy-start | bytes 388
  67.0 3.7 %copy-start.1 = (bf16[1024,4608]{1,0:T(8,128)(2,1)S(1)}, bf16[1024,4608]{1,0:T(8,128)(2,1)}, u32[]{:S(2)}) copy-start(bf16[1024,4608]{1,0:T(8,128)(2,1)} %weight_ref.1) | copy-start | bytes 28311556
  70.7 0.9 copy-start.4

commit v2 on v1

--- a/solution.py
+++ b/solution.py
@@ -9,6 +9,7 @@
 from jax.sharding import PartitionSpec as P
 
 MESH = pl.DeviceIdType.MESH
+NT = (((1,), (1,)), ((), ()))
 
 HEAD_WIDTH = 128
 
@@ -19,53 +20,210 @@
 rope_base = 10000.0
 
 
-def normed_rows(values, gain):
-    mean = jnp.mean(values * values, axis=-1, keepdims=True)
-    return values * lax.rsqrt(mean + epsilon) * gain
-
-
-def rotate(values, position):
-    half = values.shape[-1] // 2
-    freq = jnp.exp(
-        jnp.arange(half, dtype=jnp.float32) * (-2.0 * math.log(rope_base) / values.shape[-1])
-    )
-    angle = position.astype(jnp.float32)[:, None] * freq[None, :]
-    cosine = jnp.cos(angle)[:, None, :]
-    sine = jnp.sin(angle)[:, None, :]
-    first = values[..., :half]
-    second = values[..., half:]
-    return jnp.concatenate(
-        [first * cosine - second * sine, second * cosine + first * sine], axis=-1
-    )
-
-
-def attend(query, key_new, value_new, keys, values, row_cache_length):
-    scores = (
-        jnp.einsum("bgrd,bgld->bgrl", query, keys, preferred_element_type=jnp.float32)
-        * query_factor
-    )
-    own = (
-        jnp.einsum("bgrd,bgd->bgr", query, key_new, preferred_element_type=jnp.float32)
-        * query_factor
-    )
-    valid = jnp.arange(keys.shape[2])[None, :] < row_cache_length[:, None]
-    scores = jnp.where(valid[:, None, None, :], scores, -jnp.inf)
-    top = jnp.maximum(jnp.max(scores, axis=-1), own)
-    weights = jnp.exp(scores - top[..., None])
-    own_weight = jnp.exp(own - top)
-    total = jnp.sum(weights, axis=-1) + own_weight
-    probs = (weights / total[..., None]).astype(jnp.bfloat16)
-    own_prob = (own_weight / total).astype(jnp.bfloat16)
-    mixed = jnp.einsum("bgrl,bgld->bgrd", probs, values, preferred_element_type=jnp.float32)
-    mixed = (
-        mixed
-        + own_prob.astype(jnp.float32)[..., None] * value_new.astype(jnp.float32)[:, :, None, :]
-    )
-    return mixed.astype(jnp.bfloat16).reshape(query.shape[0], -1)
-
-
-NT = (((1,), (1,)), ((), ()))
-TN = (((0,), (0,)), ((), ()))
+def attention_kernel(
+    per,
+    stream_ref,
+    gain_ref,
+    length_ref,
+    query_weight_ref,
+    pair_weight_ref,
+    cache_ref,
+    out_ref,
+    normed_buf,
+    query_buf,
+    pair_buf,
+    cache_buf,
+    query_sum,
+    pair_sum,
+    query_heads,
+    key_heads,
+    value_heads,
+    length_buf,
+    query_sem,
+    pair_sem,
+    cache_sem,
+):
+    rows, width = stream_ref.shape
+    chunks, step, _ = query_buf.shape
+    pairs = key_heads.shape[0]
+    group = 128 // per
+    blocks = rows // group
+    parts = pairs * blocks
+    octets = group // 8
+    f32 = jnp.float32
+    bf16 = jnp.bfloat16
+
+    def query_copy(c):
+        return pltpu.make_async_copy(
+            query_weight_ref.at[pl.ds(c * step, step)], query_buf.at[c], query_sem.at[c]
+        )
+
+    def pair_copy(c):
+        return pltpu.make_async_copy(
+            pair_weight_ref.at[pl.ds(c * step, step)], pair_buf.at[c], pair_sem.at[c]
+        )
+
+    def cache_copy(kind, part):
+        start = pl.multiple_of((part % blocks) * group, 8)
+        return pltpu.make_async_copy(
+            cache_ref.at[kind, pl.ds(start, group), part // blocks],
+            cache_buf.at[kind, part],
+            cache_sem.at[kind, part],
+        )
+
+    for c in range(chunks):
+        pair_copy(c).start()
+        query_copy(c).start()
+
+    stream = stream_ref[...].astype(f32)
+    scale = lax.rsqrt(jnp.mean(stream * stream, axis=-1, keepdims=True) + epsilon)
+    for c in range(chunks):
+        cut = slice(c * step, (c + 1) * step)
+        normed_buf[c] = (stream[:, cut] * scale * gain_ref[:, cut].astype(f32)).astype(bf16)
+    length = jnp.broadcast_to(length_ref[...].astype(f32), (128, rows)).T
+    length_buf[...] = length
+    lane = lax.broadcasted_iota(jnp.int32, (rows, 128), 1)
+    exponent = (lane % 64).astype(f32) * (-2.0 * math.log(rope_base) / HEAD_WIDTH)
+    angle = length * jnp.exp(exponent)
+    cosine = jnp.cos(angle)
+    sine = jnp.where(lane < 64, -jnp.sin(angle), jnp.sin(angle))
+
+    near = lax.broadcasted_iota(jnp.int32, (128, 512), 0)
+    far = lax.broadcasted_iota(jnp.int32, (128, 512), 1)
+    spreader = (
+        jnp.where(far < 256, near * 2, near * 2 + 257) == far
+    ).astype(f32).astype(bf16)
+    query_sum[...] = jnp.zeros_like(query_sum)
+    pair_sum[...] = jnp.zeros_like(pair_sum)
+
+    def project(c, carry):
+        normed = normed_buf[c]
+        wide = [
+            jnp.dot(
+                normed[:, i * 128 : (i + 1) * 128], spreader, preferred_element_type=f32
+            ).astype(bf16)
+            for i in range(step // 128)
+        ]
+        both = jnp.concatenate(
+            [
+                jnp.concatenate([w[:, :256] for w in wide], axis=1),
+                jnp.concatenate([w[:, 256:] for w in wide], axis=1),
+            ],
+            axis=0,
+        )
+        pair_copy(c).wait()
+        weight = pair_buf[c].reshape(2 * step, pair_buf.shape[3])
+        pair_sum[...] += jnp.dot(both, weight, preferred_element_type=f32)
+        query_copy(c).wait()
+        query_sum[...] += jnp.dot(normed, query_buf[c], preferred_element_type=f32)
+
+        @pl.when(c < parts)
+        def _():
+            cache_copy(0, c).start()
+            cache_copy(1, c).start()
+
+        return carry
+
+    lax.fori_loop(0, chunks, project, 0)
+
+    def turned(values):
+        return values * cosine + pltpu.roll(values, 64, 1) * sine
+
+    for h in range(pairs * per):
+        query_heads[h] = turned(query_sum[:, h * 128 : (h + 1) * 128]).astype(bf16)
+    for g in range(pairs):
+        cut = slice(g * 128, (g + 1) * 128)
+        key_heads[g] = turned(pair_sum[0:rows, cut]).astype(bf16)
+        value_heads[g] = pair_sum[rows : 2 * rows, cut].astype(bf16)
+
+    def stacked(pieces):
+        return jnp.stack([p.reshape(octets, 8, 128) for p in pieces], axis=1).reshape(128, 128)
+
+    def attend_part(part, carry):
+        g = part // blocks
+        start = pl.multiple_of((part % blocks) * group, 8)
+        here = pl.ds(start, group)
+        query = stacked([query_heads[g * per + i, here].astype(f32) for i in range(per)])
+        key_new = stacked([key_heads[g, here].astype(f32)] * per)
+        value_new = stacked([value_heads[g, here].astype(f32)] * per)
+        limit = stacked([length_buf[here]] * per)
+        own = jnp.sum(query * key_new, axis=1, keepdims=True) * query_factor
+        query = query.astype(bf16)
+        across = lax.broadcasted_iota(jnp.int32, (128, 128), 1)
+        row_of_lane = (across // (8 * per)) * 8 + across % 8
+        scores = jnp.zeros((128, 128), f32)
+        cache_copy(0, part).wait()
+        for j in range(octets):
+            keys = cache_buf[0, part, 8 * j : 8 * j + 8].reshape(1024, 128)
+            product = lax.dot_general(keys, query, NT, preferred_element_type=f32)
+            for r in range(8):
+                scores = jnp.where(
+                    row_of_lane == 8 * j + r, product[128 * r : 128 * (r + 1)], scores
+                )
+        scores = scores.T * query_factor
+        scores = jnp.where(across.astype(f32) < limit, scores, -jnp.inf)
+        top = jnp.maximum(jnp.max(scores, axis=1, keepdims=True), own)
+        weights = jnp.exp(scores - top)
+        own_weight = jnp.exp(own - top)
+        total = jnp.sum(weights, axis=1, keepdims=True) + own_weight
+        probs = weights / total
+        own_prob = (own_weight / total).astype(bf16).astype(f32)
+        tall = 8 * per
+        row_in_octet = lax.broadcasted_iota(jnp.int32, (tall, 128), 0) % 8
+        mixed = []
+        cache_copy(1, part).wait()
+        for j in range(octets):
+            piece = probs[tall * j : tall * (j + 1)]
+            spread = jnp.concatenate(
+                [jnp.where(row_in_octet == r, piece, 0.0).astype(bf16) for r in range(8)], axis=1
+            )
+            values = cache_buf[1, part, 8 * j : 8 * j + 8].reshape(1024, 128)
+            mixed.append(jnp.dot(spread, values, preferred_element_type=f32))
+        mixed = jnp.concatenate(mixed, axis=0) + own_prob * value_new
+        mixed = mixed.astype(bf16).astype(f32).reshape(octets, per, 8, 128)
+        for i in range(per):
+            column = pl.multiple_of((g * per + i) * 128, 128)
+            out_ref[here, pl.ds(column, 128)] = mixed[:, i].reshape(group, 128).astype(bf16)
+        return carry
+
+    lax.fori_loop(0, parts, attend_part, 0)
+
+
+def attention(stream, gain, lengths, query_weight, pair_weight, cache):
+    rows, width = stream.shape
+    step = 512
+    chunks = width // step
+    pairs = pair_weight.shape[2] // HEAD_WIDTH
+    heads = query_weight.shape[1] // HEAD_WIDTH
+    per = heads // pairs
+    group = 128 // per
+    parts = pairs * (rows // group)
+    bf16 = jnp.bfloat16
+    dma = pltpu.SemaphoreType.DMA
+    vmem = pl.BlockSpec(memory_space=pltpu.VMEM)
+    hbm = pl.BlockSpec(memory_space=pl.ANY)
+    return pl.pallas_call(
+        functools.partial(attention_kernel, per),
+        out_shape=jax.ShapeDtypeStruct((rows, heads * HEAD_WIDTH), bf16),
+        in_specs=[vmem] * 3 + [hbm] * 3,
+        out_specs=vmem,
+        scratch_shapes=[
+            pltpu.VMEM((chunks, rows, step), bf16),
+            pltpu.VMEM((chunks, step, heads * HEAD_WIDTH), bf16),
+            pltpu.VMEM((chunks, step, 2, pairs * HEAD_WIDTH), bf16),
+            pltpu.VMEM((2, parts, group, cache.shape[3], HEAD_WIDTH), bf16),
+            pltpu.VMEM((rows, heads * HEAD_WIDTH), jnp.float32),
+            pltpu.VMEM((2 * rows, pairs * HEAD_WIDTH), jnp.float32),
+            pltpu.VMEM((heads, rows, HEAD_WIDTH), bf16),
+            pltpu.VMEM((pairs, rows, HEAD_WIDTH), bf16),
+            pltpu.VMEM((pairs, rows, HEAD_WIDTH), bf16),
+            pltpu.VMEM((rows, HEAD_WIDTH), jnp.float32),
+            dma((chunks,)),
+            dma((chunks,)),
+            dma((2, parts)),
+        ],
+        compiler_params=pltpu.CompilerParams(vmem_limit_bytes=60 << 20),
+    )(stream, gain.reshape(1, -1), lengths.reshape(1, -1), query_weight, pair_weight, cache)
 
 
 def exchange_kernel(
@@ -404,21 +562,13 @@
     rank_padding = adapter_down_weight.shape[2]
     adapter_portion = adapter_up_weight.shape[2]
     capacity = row_count // 4
-    heads_local = query_projection.shape[1] // HEAD_WIDTH
-    pairs_local = key_value_weight.shape[2] // HEAD_WIDTH
-    stream_f = stream.astype(jnp.float32)
-    normed = normed_rows(stream_f, input_norm_gain.astype(jnp.float32)).astype(jnp.bfloat16)
-    query = jnp.dot(normed, query_projection, preferred_element_type=jnp.float32).reshape(
-        row_count, heads_local, HEAD_WIDTH
-    )
-    query = rotate(query, row_cache_length).astype(jnp.bfloat16)
-    query = query.reshape(row_count, pairs_local, heads_local // pairs_local, HEAD_WIDTH)
-    pair = jnp.dot(normed, key_value_weight.reshape(width, -1), preferred_element_type=jnp.float32)
-    pair = pair.reshape(row_count, 2, pairs_local, HEAD_WIDTH)
-    key_new = rotate(pair[:, 0], row_cache_length).astype(jnp.bfloat16)
-    value_new = pair[:, 1].astype(jnp.bfloat16)
-    mixed = attend(
-        query, key_new, value_new, cached_key_value[0], cached_key_value[1], row_cache_length
+    mixed = attention(
+        stream,
+        input_norm_gain,
+        row_cache_length,
+        query_projection,
+        key_value_weight,
+        cached_key_value,
     )
     if lax.axis_size("tensor") == 4 and adapter_portion % 128 == 0 and row_count == 128:
         return exchange(
@@ -432,6 +582,7 @@
             stream,
             output_projection,
         )
+    stream_f = stream.astype(jnp.float32)
     adapters = adapter_slot_table.shape[0]
     match = row_adapter_index[:, None] == jnp.arange(adapters)[None, :]
     slot = jnp.sum(jnp.where(match, adapter_slot_table[None, :], 0), axis=1)

time: 103 us -> 62 us (0.60)
  matrix products: 32.2 us -> 0 us
  local copies, waits for them, and re-layouts: 34 us -> 7.37 us
  Pallas kernels: 29.7 us -> 54.3 us
  other arithmetic: 5.87 us -> 0 us
    dot_general x4 -> x0, matrix products: 32.2 us -> none  [the longest x1 12.6 us: attend(): jnp.einsum('bgrd,bgld->bgrl', query, keys, preferred_element_type=jnp.flo...]
    pallas_call x0 -> x1, Pallas kernels: none -> 24.8 us  [attention(): pl.pallas_call(functools.partial(attention_kernel, per), out_shape=jax.Sh...]
    dot_general x2 -> x0, local copies, waits for them, and re-layouts: 13 us -> none  [the longest x1 12.9 us: per_device(): jnp.dot(normed, key_value_weight.reshape(width, -1), preferred_element_ty...]
    unnamed x28 -> x17, local copies, waits for them, and re-layouts: 16 us -> 5.37 us
    reduce_sum x2 -> x0, other arithmetic: 2.94 us -> none  [the longest x1 1.58 us: normed_rows(): mean = jnp.mean(values * values, axis=-1, keepdims=True)]
    convert_element_type x2 -> x0, local copies, waits for them, and re-layouts: 1.68 us -> none  [the longest x1 0.85 us: attend(): own_prob.astype(jnp.float32)[..., None]]
    unnamed x2 -> x0, other arithmetic: 1.52 us -> none
where the time goes in v2:
time: 62 us; the launch traced here: 61.8 us
  Pallas kernels  54.3 us (88%)
  local copies, waits for them, and re-layouts  7.37 us (12%)
    pallas_call x1, Pallas kernels, exchange(): pl.pallas_call(functools.partial(exchange_kernel, stores, column_count, k...  29.5 us
    pallas_call x1, Pallas kernels, attention(): pl.pallas_call(functools.partial(attention_kernel, per), out_shape=jax.Sh...  24.8 us
    unnamed x17, local copies, waits for them, and re-layouts  5.37 us
    reshape x1, local copies, waits for them, and re-layouts, attention(): gain.reshape(1, -1)  1.31 us

profile of v2, /device:TPU:0, one launch (start us, length us, event | category | flops | bytes accessed | tf_op | source)
XLA Modules:
  0.0 61.8 jit_solution(394307195784761626)
XLA Ops:
  0.0 0.7 %reshape.31.gain_ref = bf16[1,1152]{1,0:T(2,128)(2,1)S(1)} reshape(bf16[1152]{0:T(1024)(128)(2,1)} %param.15) | data formatting | bytes 4608 | tf_op jit(solution)/shard_map/reshape | solution.py:537
  0.7 1.3 %reshape.24.gain_ref = bf16[1,4608]{1,0:T(2,128)(2,1)} reshape(bf16[4608]{0:T(1024)(128)(2,1)} %param.14) | data formatting | bytes 18432 | tf_op jit(solution)/shard_map/reshape | solution.py:226
  2.0 0.0 copy-start.1
  2.0 0.0 copy-start.2
  2.0 0.0 copy-start.4
  2.0 0.0 copy-start.5
  2.0 0.0 copy-start.6
  2.0 0.0 copy-start.7
  2.0 24.8 %shard_map.127.mixed_ref = bf16[128,1024]{1,0:T(8,128)(2,1)} custom-call(bf16[128,4608]{1,0:T(8,128)(2,1)} %stream_ref.3, bf16[1,4608]{1,0:T(2,128)(2,1)} %reshape.24.gain_ref, s32[1,128]{1,0:T(1,128)} %bitcast.13, bf16[4608,1024]{1,0:T(8,128)(2,1)} %query_weight_ref.1, bf16[4608,2,512]{2,1,0:T(2,128)(2,1)} %pair_weight_ref.1, ...), custom_call_target="tpu_custom_call" | custom-call | tf_op jit(solution)/shard_map/pallas_call | solution.py:205
  26.9 0.0 copy-done.1
  26.9 0.0 copy-done.2
  26.9 0.0 copy-done.4
  26.9 0.0 copy-done.5
  26.9 0.0 copy-done.6
  26.9 0.0 copy-done.7
  26.9 0.0 copy-start
  26.9 3.7 %copy-done = bf16[1024,4608]{1,0:T(8,128)(2,1)S(1)} copy-done((bf16[1024,4608]{1,0:T(8,128)(2,1)S(1)}, bf16[1024,4608]{1,0:T(8,128)(2,1)}, u32[]{:S(2)}) %copy-start) | copy-done | bytes 9437208
  30.6 0.0 copy-start.3
  30.6 0.9 %copy-done.3 = bf16[128,1024]{1,0:T(8,128)(2,1)S(1)} copy-done((bf16[128,1024]{1,0:T(8,128)(2,1)S(1)}, bf16[128,1024]{1,0:T(8,128)(2,1)}, u32[]{:S(2)}) %copy-start.3) | copy-done | bytes 262168
  31.6 29.5 %shard_map.128 = bf16[128,1152]{1,0:T(8,128)(2,1)S(1)} custom-call(bf16[128,1024]{1,0:T(8,128)(2,1)S(1)} %copy-done.3, s32[1,128]{1,0:T(1,128)S(1)} %bitcast.10, s32[1,32]{1,0:T(1,128)S(1)} %bitcast.11, s32[1,32]{1,0:T(1,128)S(1)} %bitcast.12, bf16[512,1024]{1,0:T(8,128)(2,1)S(1)} %bitcast.9, bf16[512,1152]{1,0:T(8,128)(2,1)S(1)} %bitcast.8, ...), custom_call_target="tpu_custom_call" | custom-call | tf_op jit(solution)/shard_map/pallas_call | solution.py:495
  61.1 0.7 %copy.15 = bf16[128,1152]{1,0:T(8,128)(2,1)} copy(bf16[128,1152]{1,0:T(8,128)(2,1)S(1)} %shard_map.128) | data formatting | bytes 589824
Async XLA Ops:
  2.0 24.9 %copy-start.1 = (bf16[128,4608]{1,0:T(8,128)(2,1)S(1)}, bf16[128,4608]{1,0:T(8,128)(2,1)}, u32[]{:S(2)}) copy-start(bf16[128,4608]{1,0:T(8,128)(2,1)} %stream_ref.3) | copy-start | bytes 3538948
  2.0 24.9 %copy-start.2 = (bf16[8,64,1152]{2,1,0:T(8,128)(2,1)S(1)}, bf16[8,64,1152]{2,1,0:T(8,128)(2,1)}, u32[]{:S(2)}) copy-start(bf16[8,64,1152]{2,1,0:T(8,128)(2,1)} %param.25) | copy-start | bytes 3538948
  2.0 24.9 %copy-start.4 = (bf16[1024,8,64]{0,2,1:T(8,128)(2,1)S(1)}, bf16[1024,8,64]{0,2,1:T(8,128)(2,1)}, u32[]{:S(2)}) copy-start(bf16[1024,8,64]{0,2,1:T(8,128)(2,1)} %param.24) | copy-start | bytes 3145732
  2.0 24.9 %copy-start.5 = (s32[128]{0:T(128)S(1)}, s32[128]{0:T(128)}, u32[]{:S(2)}) copy-start(s32[128]{0:T(128)} %param.21) | copy-start | bytes 1540
  2.0 24.9 %copy-start.6 = (s32[32]{0:T(128)S(1)}, s32[32]{0:T(128)}, u32[]{:S(2)}) copy-start(s32[32]{0:T(128)} %param.22) | copy-start | bytes 388
  2.0 24.9 %copy-start.7 = (s32[32]{0:T(128)S(1)}, s32[32]{0:T(128)}, u32[]{:S(2)}) copy-start(s32[32]{0:T(128)} %param.23) | copy-start | bytes 388
  26.9 3.7 %copy-start = (bf16[1024,4608]{1,0:T(8,128)(2,1)S(1)}, bf16[1024,4608]{1,0:T(8,128)(2,1)}, u32[]{:S(2)}) copy-start(bf16[1024,4608]{1,0:T(8,128)(2,1)} %weight_ref.1) | copy-start | bytes 28311556
  30.6 0.9 %copy-start.3 = (bf16[128,1024]{1,0:T(8,128)(2,1)S(1)}, bf16[128,1024]{1,0:T(8,128)(2,1)}, u32[]{:S(2)}) copy-start(bf16[128,1024]{1,0:T(8,128)(2,1)} %shard_map.127.mixed_ref) | copy-start | bytes 786436

commit v3 on v2

--- a/solution.py
+++ b/solution.py
@@ -22,6 +22,9 @@
 
 def attention_kernel(
     per,
+    begin,
+    after_weights,
+    after_group,
     stream_ref,
     gain_ref,
     length_ref,
@@ -29,6 +32,7 @@
     pair_weight_ref,
     cache_ref,
     out_ref,
+    stream_buf,
     normed_buf,
     query_buf,
     pair_buf,
@@ -42,8 +46,10 @@
     query_sem,
     pair_sem,
     cache_sem,
+    stream_sem,
 ):
-    rows, width = stream_ref.shape
+    rows, width = stream_buf.shape
+    slots = cache_buf.shape[1]
     chunks, step, _ = query_buf.shape
     pairs = key_heads.shape[0]
     group = 128 // per
@@ -67,15 +73,19 @@
         start = pl.multiple_of((part % blocks) * group, 8)
         return pltpu.make_async_copy(
             cache_ref.at[kind, pl.ds(start, group), part // blocks],
-            cache_buf.at[kind, part],
-            cache_sem.at[kind, part],
-        )
-
+            cache_buf.at[kind, part % slots],
+            cache_sem.at[kind, part % slots],
+        )
+
+    stream_copy = pltpu.make_async_copy(stream_ref, stream_buf, stream_sem)
+    stream_copy.start()
     for c in range(chunks):
         pair_copy(c).start()
         query_copy(c).start()
-
-    stream = stream_ref[...].astype(f32)
+    if begin is not None:
+        begin()
+    stream_copy.wait()
+    stream = stream_buf[...].astype(f32)
     scale = lax.rsqrt(jnp.mean(stream * stream, axis=-1, keepdims=True) + epsilon)
     for c in range(chunks):
         cut = slice(c * step, (c + 1) * step)
@@ -117,7 +127,7 @@
         query_copy(c).wait()
         query_sum[...] += jnp.dot(normed, query_buf[c], preferred_element_type=f32)
 
-        @pl.when(c < parts)
+        @pl.when(c < slots)
         def _():
             cache_copy(0, c).start()
             cache_copy(1, c).start()
@@ -125,6 +135,8 @@
         return carry
 
     lax.fori_loop(0, chunks, project, 0)
+    if after_weights is not None:
+        after_weights()
 
     def turned(values):
         return values * cosine + pltpu.roll(values, 64, 1) * sine
@@ -152,9 +164,10 @@
         across = lax.broadcasted_iota(jnp.int32, (128, 128), 1)
         row_of_lane = (across // (8 * per)) * 8 + across % 8
         scores = jnp.zeros((128, 128), f32)
+        slot = part % slots
         cache_copy(0, part).wait()
         for j in range(octets):
-            keys = cache_buf[0, part, 8 * j : 8 * j + 8].reshape(1024, 128)
+            keys = cache_buf[0, slot, 8 * j : 8 * j + 8].reshape(1024, 128)
             product = lax.dot_general(keys, query, NT, preferred_element_type=f32)
             for r in range(8):
                 scores = jnp.where(
@@ -177,51 +190,70 @@
             spread = jnp.concatenate(
                 [jnp.where(row_in_octet == r, piece, 0.0).astype(bf16) for r in range(8)], axis=1
             )
-            values = cache_buf[1, part, 8 * j : 8 * j + 8].reshape(1024, 128)
+            values = cache_buf[1, slot, 8 * j : 8 * j + 8].reshape(1024, 128)
             mixed.append(jnp.dot(spread, values, preferred_element_type=f32))
         mixed = jnp.concatenate(mixed, axis=0) + own_prob * value_new
         mixed = mixed.astype(bf16).astype(f32).reshape(octets, per, 8, 128)
         for i in range(per):
             column = pl.multiple_of((g * per + i) * 128, 128)
             out_ref[here, pl.ds(column, 128)] = mixed[:, i].reshape(group, 128).astype(bf16)
+
+        @pl.when(part + slots < parts)
+        def _():
+            cache_copy(0, part + slots).start()
+            cache_copy(1, part + slots).start()
+
+        if after_group is not None:
+
+            @pl.when(part % blocks == blocks - 1)
+            def _():
+                after_group(g)
+
         return carry
 
     lax.fori_loop(0, parts, attend_part, 0)
 
 
-def attention(stream, gain, lengths, query_weight, pair_weight, cache):
-    rows, width = stream.shape
+def attention_scratch(rows, width, query_weight, pair_weight, cache):
     step = 512
     chunks = width // step
     pairs = pair_weight.shape[2] // HEAD_WIDTH
     heads = query_weight.shape[1] // HEAD_WIDTH
-    per = heads // pairs
-    group = 128 // per
-    parts = pairs * (rows // group)
+    group = 128 * pairs // heads
+    slots = min(pairs * (rows // group), 5)
     bf16 = jnp.bfloat16
     dma = pltpu.SemaphoreType.DMA
+    return [
+        pltpu.VMEM((rows, width), bf16),
+        pltpu.VMEM((chunks, rows, step), bf16),
+        pltpu.VMEM((chunks, step, heads * HEAD_WIDTH), bf16),
+        pltpu.VMEM((chunks, step, 2, pairs * HEAD_WIDTH), bf16),
+        pltpu.VMEM((2, slots, group, cache.shape[3], HEAD_WIDTH), bf16),
+        pltpu.VMEM((rows, heads * HEAD_WIDTH), jnp.float32),
+        pltpu.VMEM((2 * rows, pairs * HEAD_WIDTH), jnp.float32),
+        pltpu.VMEM((heads, rows, HEAD_WIDTH), bf16),
+        pltpu.VMEM((pairs, rows, HEAD_WIDTH), bf16),
+        pltpu.VMEM((pairs, rows, HEAD_WIDTH), bf16),
+        pltpu.VMEM((rows, HEAD_WIDTH), jnp.float32),
+        dma((chunks,)),
+        dma((chunks,)),
+        dma((2, slots)),
+        dma,
+    ]
+
+
+def attention(stream, gain, lengths, query_weight, pair_weight, cache):
+    rows, width = stream.shape
+    heads = query_weight.shape[1] // HEAD_WIDTH
+    per = query_weight.shape[1] // pair_weight.shape[2]
     vmem = pl.BlockSpec(memory_space=pltpu.VMEM)
     hbm = pl.BlockSpec(memory_space=pl.ANY)
     return pl.pallas_call(
-        functools.partial(attention_kernel, per),
-        out_shape=jax.ShapeDtypeStruct((rows, heads * HEAD_WIDTH), bf16),
-        in_specs=[vmem] * 3 + [hbm] * 3,
+        functools.partial(attention_kernel, per, None, None, None),
+        out_shape=jax.ShapeDtypeStruct((rows, heads * HEAD_WIDTH), jnp.bfloat16),
+        in_specs=[hbm] + [vmem] * 2 + [hbm] * 3,
         out_specs=vmem,
-        scratch_shapes=[
-            pltpu.VMEM((chunks, rows, step), bf16),
-            pltpu.VMEM((chunks, step, heads * HEAD_WIDTH), bf16),
-            pltpu.VMEM((chunks, step, 2, pairs * HEAD_WIDTH), bf16),
-            pltpu.VMEM((2, parts, group, cache.shape[3], HEAD_WIDTH), bf16),
-            pltpu.VMEM((rows, heads * HEAD_WIDTH), jnp.float32),
-            pltpu.VMEM((2 * rows, pairs * HEAD_WIDTH), jnp.float32),
-            pltpu.VMEM((heads, rows, HEAD_WIDTH), bf16),
-            pltpu.VMEM((pairs, rows, HEAD_WIDTH), bf16),
-            pltpu.VMEM((pairs, rows, HEAD_WIDTH), bf16),
-            pltpu.VMEM((rows, HEAD_WIDTH), jnp.float32),
-            dma((chunks,)),
-            dma((chunks,)),
-            dma((2, parts)),
-        ],
+        scratch_shapes=attention_scratch(rows, width, query_weight, pair_weight, cache),
         compiler_params=pltpu.CompilerParams(vmem_limit_bytes=60 << 20),
     )(stream, gain.reshape(1, -1), lengths.reshape(1, -1), query_weight, pair_weight, cache)
 
@@ -231,20 +263,31 @@
     column_count,
     kept,
     capacity,
-    mixed_ref,
+    per,
+    input_gain_ref,
+    length_ref,
     index_ref,
     slot_ref,
     rank_ref,
+    gain_ref,
+    stream_ref,
+    query_weight_ref,
+    pair_weight_ref,
+    cache_ref,
     down_ref,
     up_ref,
-    gain_ref,
-    stream_ref,
     weight_ref,
     out_ref,
+    mixed_ref,
+    down_buf,
+    up_buf,
+    packer_buf,
     weight_buf,
     stream_buf,
     out_buf,
     in_buf,
+    label_buf,
+    label_in,
     part_buf,
     part_in,
     cross_buf,
@@ -258,6 +301,8 @@
     load_sem,
     row_send,
     row_recv,
+    label_send,
+    label_recv,
     part_send,
     part_recv,
     low_send,
@@ -266,10 +311,13 @@
     back_recv,
     stat_send,
     stat_recv,
+    *attention_refs,
 ):
     rows, depth = mixed_ref.shape
     portion = gain_ref.shape[1]
     rank_width = down_ref.shape[0] // kept
+    pairs = out_buf.shape[1]
+    span = depth // pairs
     width = portion * column_count
     f32 = jnp.float32
     bf16 = jnp.bfloat16
@@ -295,69 +343,107 @@
             stream_ref.at[:, pl.ds(mine, portion)], stream_buf, load_sem.at[column_count]
         )
     )
-    for load in loads:
-        load.start()
-
-    barrier = pltpu.get_barrier_semaphore()
-    for k in range(1, stores):
-        pl.semaphore_signal(
-            barrier, inc=1, device_id={"store": (store + k) % stores}, device_id_type=MESH
-        )
-    for k in range(1, column_count):
-        pl.semaphore_signal(
-            barrier, inc=1, device_id={"tensor": (column + k) % column_count}, device_id_type=MESH
-        )
-
-    adapters = slot_ref.shape[1]
-    match = (
-        lax.broadcasted_iota(jnp.int32, (adapters, rows), 0) == index_ref[...]
-    ).astype(f32)
-    slot = jnp.dot(
-        jnp.broadcast_to(slot_ref[...].astype(f32), (8, adapters)), match, preferred_element_type=f32
-    )
-    rank = jnp.dot(
-        jnp.broadcast_to(rank_ref[...].astype(f32), (8, adapters)), match, preferred_element_type=f32
-    )
-    owner = jnp.zeros((8, rows), f32)
-    for s in range(1, stores):
-        owner = owner + (slot >= float(s * kept)).astype(f32)
-    within = slot - owner * float(kept)
-    turned = owner - store.astype(f32)
-    turned = jnp.where(turned < 0.0, turned + float(stores), turned)
-    target = (lax.broadcasted_iota(jnp.int32, (8, rows), 0).astype(f32) == turned).astype(f32)
-    earlier = (
-        lax.broadcasted_iota(jnp.int32, (rows, rows), 0)
-        < lax.broadcasted_iota(jnp.int32, (rows, rows), 1)
-    ).astype(f32)
-    before = jnp.dot(target, earlier, preferred_element_type=f32)
-    place = jnp.sum(before * target, axis=0, keepdims=True) + turned[0:1] * float(capacity)
-    packer_f = (
-        lax.broadcasted_iota(jnp.int32, (stores * capacity, rows), 0).astype(f32) == place
-    ).astype(f32)
-    packer = packer_f.astype(bf16)
-    line = lax.broadcasted_iota(jnp.int32, (128, rows), 0)
-    labels = jnp.where(line == 0, within[0:1] + 1.0, jnp.where(line == 1, rank[0:1], 0.0))
-    labels = lax.dot_general(packer, labels.astype(bf16), NT, preferred_element_type=f32)
-    mixed = mixed_ref[...]
-    outgoing = jnp.dot(packer, mixed, preferred_element_type=f32)
-    out_buf[:, :, 0:depth] = outgoing.astype(bf16).reshape(stores, capacity, depth)
-    out_buf[:, :, depth : depth + 128] = labels.astype(bf16).reshape(stores, capacity, 128)
-
-    pl.semaphore_wait(barrier, stores + column_count - 2)
-
-    def row_copy(k):
+    loads.append(pltpu.make_async_copy(down_ref, down_buf, load_sem.at[column_count + 1]))
+    loads.append(pltpu.make_async_copy(up_ref, up_buf, load_sem.at[column_count + 2]))
+
+    def label_copy(k):
         return pltpu.make_async_remote_copy(
-            src_ref=out_buf.at[k],
-            dst_ref=in_buf.at[k - 1],
-            send_sem=row_send.at[k - 1],
-            recv_sem=row_recv.at[k - 1],
+            src_ref=label_buf.at[k],
+            dst_ref=label_in.at[k - 1],
+            send_sem=label_send.at[k - 1],
+            recv_sem=label_recv.at[k - 1],
             device_id={"store": (store + k) % stores},
             device_id_type=MESH,
         )
 
-    row_copies = [row_copy(k) for k in range(1, stores)]
-    for copy in row_copies:
-        copy.start()
+    def row_copy(k, g):
+        return pltpu.make_async_remote_copy(
+            src_ref=out_buf.at[k, g],
+            dst_ref=in_buf.at[k - 1, g],
+            send_sem=row_send.at[k - 1, g],
+            recv_sem=row_recv.at[k - 1, g],
+            device_id={"store": (store + k) % stores},
+            device_id_type=MESH,
+        )
+
+    barrier = pltpu.get_barrier_semaphore()
+
+    def begin():
+        for k in range(1, stores):
+            pl.semaphore_signal(
+                barrier, inc=1, device_id={"store": (store + k) % stores}, device_id_type=MESH
+            )
+        for k in range(1, column_count):
+            pl.semaphore_signal(
+                barrier, inc=1, device_id={"tensor": (column + k) % column_count}, device_id_type=MESH
+            )
+
+        adapters = slot_ref.shape[1]
+        match = (
+            lax.broadcasted_iota(jnp.int32, (adapters, rows), 0) == index_ref[...]
+        ).astype(f32)
+        slot = jnp.dot(
+            jnp.broadcast_to(slot_ref[...].astype(f32), (8, adapters)), match, preferred_element_type=f32
+        )
+        rank = jnp.dot(
+            jnp.broadcast_to(rank_ref[...].astype(f32), (8, adapters)), match, preferred_element_type=f32
+        )
+        owner = jnp.zeros((8, rows), f32)
+        for s in range(1, stores):
+            owner = owner + (slot >= float(s * kept)).astype(f32)
+        within = slot - owner * float(kept)
+        turned = owner - store.astype(f32)
+        turned = jnp.where(turned < 0.0, turned + float(stores), turned)
+        target = (lax.broadcasted_iota(jnp.int32, (8, rows), 0).astype(f32) == turned).astype(f32)
+        earlier = (
+            lax.broadcasted_iota(jnp.int32, (rows, rows), 0)
+            < lax.broadcasted_iota(jnp.int32, (rows, rows), 1)
+        ).astype(f32)
+        before = jnp.dot(target, earlier, preferred_element_type=f32)
+        place = jnp.sum(before * target, axis=0, keepdims=True) + turned[0:1] * float(capacity)
+        packer_f = (
+            lax.broadcasted_iota(jnp.int32, (stores * capacity, rows), 0).astype(f32) == place
+        ).astype(f32)
+        packer = packer_f.astype(bf16)
+        packer_buf[...] = packer
+        line = lax.broadcasted_iota(jnp.int32, (128, rows), 0)
+        labels = jnp.where(line == 0, within[0:1] + 1.0, jnp.where(line == 1, rank[0:1], 0.0))
+        labels = lax.dot_general(packer, labels.astype(bf16), NT, preferred_element_type=f32)
+        label_buf[...] = labels.astype(bf16).reshape(stores, capacity, 128)
+
+    def after_weights():
+        pl.semaphore_wait(barrier, stores + column_count - 2)
+        for k in range(1, stores):
+            label_copy(k).start()
+        for load in loads:
+            load.start()
+
+    def send_group(g):
+        start = pl.multiple_of(g * span, 128)
+        outgoing = jnp.dot(
+            packer_buf[...], mixed_ref[:, pl.ds(start, span)], preferred_element_type=f32
+        )
+        outgoing = outgoing.astype(bf16)
+        for k in range(stores):
+            out_buf[k, g] = outgoing[k * capacity : (k + 1) * capacity]
+        for k in range(1, stores):
+            row_copy(k, g).start()
+
+    attention_kernel(
+        per,
+        begin,
+        after_weights,
+        send_group,
+        stream_ref,
+        input_gain_ref,
+        length_ref,
+        query_weight_ref,
+        pair_weight_ref,
+        cache_ref,
+        mixed_ref,
+        *attention_refs,
+    )
+    mixed = mixed_ref[...]
 
     part_copies = []
     for i in range(2):
@@ -387,12 +473,21 @@
     )
     cross_copy.start()
 
-    for copy in row_copies:
-        copy.wait()
-    block = jnp.concatenate([out_buf[0]] + [in_buf[k] for k in range(stores - 1)], axis=0)
-    code = block[:, depth : depth + 1].astype(f32)
-    row_rank = block[:, depth + 1 : depth + 2].astype(f32)
-    full = lax.dot_general(block[:, 0:depth], down_ref[...], NT, preferred_element_type=f32)
+    for k in range(1, stores):
+        label_copy(k).wait()
+    label = jnp.concatenate([label_buf[0]] + [label_in[k] for k in range(stores - 1)], axis=0)
+    code = label[:, 0:1].astype(f32)
+    row_rank = label[:, 1:2].astype(f32)
+    loads[5].wait()
+    loads[6].wait()
+    full = jnp.zeros((stores * capacity, kept * rank_width), f32)
+    for g in range(pairs):
+        for k in range(1, stores):
+            row_copy(k, g).wait()
+        block = jnp.concatenate([out_buf[0, g]] + [in_buf[k, g] for k in range(stores - 1)], axis=0)
+        full = full + lax.dot_general(
+            block, down_buf[:, g * span : (g + 1) * span], NT, preferred_element_type=f32
+        )
     count = stores * capacity
     lane = lax.broadcasted_iota(jnp.int32, (count, kept * rank_width), 1).astype(f32)
     choose = jnp.logical_and(
@@ -429,7 +524,7 @@
     narrow = jnp.where(live, coordinates * (adapter_strength / jnp.maximum(row_rank, 1.0)), 0.0)
     spread = jnp.concatenate([narrow] * (kept * rank_width // 128), axis=1)
     spread = jnp.where(choose, spread, 0.0).astype(bf16)
-    wide = jnp.dot(spread, up_ref[...], preferred_element_type=f32).astype(bf16)
+    wide = jnp.dot(spread, up_buf[...], preferred_element_type=f32).astype(bf16)
     back_buf[...] = wide.reshape(stores, capacity, portion)
     back_copies = []
     for k in range(1, stores):
@@ -444,7 +539,7 @@
         copy.start()
         back_copies.append(copy)
 
-    unpacker = packer_f.T.astype(bf16)
+    unpacker = packer_buf[...].astype(f32).T.astype(bf16)
     cross_copy.wait()
     own = own + cross_in[...].astype(f32)
     for copy in back_copies:
@@ -478,10 +573,29 @@
     ).astype(bf16)
 
 
-def exchange(mixed, index, slots, ranks, down, up, gain, stream, weight):
+def exchange(
+    stream,
+    input_gain,
+    lengths,
+    query_weight,
+    pair_weight,
+    cache,
+    index,
+    slots,
+    ranks,
+    down,
+    up,
+    gain,
+    weight,
+):
     stores = lax.axis_size("store")
     column_count = lax.axis_size("tensor")
-    rows, depth = mixed.shape
+    rows, width = stream.shape
+    depth = query_weight.shape[1]
+    per = depth // pair_weight.shape[2]
+    pairs = pair_weight.shape[2] // HEAD_WIDTH
+    span = depth // pairs
+    own_scratch = attention_scratch(rows, width, query_weight, pair_weight, cache)
     kept = down.shape[1]
     rank_width = down.shape[2]
     portion = up.shape[2]
@@ -493,15 +607,23 @@
     vmem = pl.BlockSpec(memory_space=pltpu.VMEM)
     hbm = pl.BlockSpec(memory_space=pl.ANY)
     return pl.pallas_call(
-        functools.partial(exchange_kernel, stores, column_count, kept, capacity),
+        functools.partial(
+            exchange_kernel, stores, column_count, kept, capacity, per
+        ),
         out_shape=jax.ShapeDtypeStruct((rows, portion), bf16),
-        in_specs=[vmem] * 7 + [hbm] * 2,
+        in_specs=[vmem] * 6 + [hbm] * 7,
         out_specs=vmem,
         scratch_shapes=[
+            pltpu.VMEM((rows, depth), bf16),
+            pltpu.VMEM((kept * rank_width, depth), bf16),
+            pltpu.VMEM((kept * rank_width, portion), bf16),
+            pltpu.VMEM((stores * capacity, rows), bf16),
             pltpu.VMEM((column_count, depth, portion), bf16),
             pltpu.VMEM((rows, portion), bf16),
-            pltpu.VMEM((stores, capacity, depth + 128), bf16),
-            pltpu.VMEM((stores - 1, capacity, depth + 128), bf16),
+            pltpu.VMEM((stores, pairs, capacity, span), bf16),
+            pltpu.VMEM((stores - 1, pairs, capacity, span), bf16),
+            pltpu.VMEM((stores, capacity, 128), bf16),
+            pltpu.VMEM((stores - 1, capacity, 128), bf16),
             pltpu.VMEM((2, rows, portion), bf16),
             pltpu.VMEM((2, rows, portion), bf16),
             pltpu.VMEM((rows, portion), bf16),
@@ -512,7 +634,9 @@
             pltpu.VMEM((stores - 1, capacity, portion), bf16),
             pltpu.VMEM((8, rows), jnp.float32),
             pltpu.VMEM((column_count - 1, 8, rows), jnp.float32),
-            dma((column_count + 1,)),
+            dma((column_count + 3,)),
+            dma((stores - 1, pairs)),
+            dma((stores - 1, pairs)),
             dma((stores - 1,)),
             dma((stores - 1,)),
             dma((3,)),
@@ -523,19 +647,24 @@
             dma((stores - 1,)),
             dma((column_count - 1,)),
             dma((column_count - 1,)),
-        ],
+        ]
+        + own_scratch,
         compiler_params=pltpu.CompilerParams(
-            collective_id=0, has_side_effects=True, vmem_limit_bytes=40 << 20
+            collective_id=0, has_side_effects=True, vmem_limit_bytes=62 << 20
         ),
     )(
-        mixed,
+        input_gain.reshape(1, -1),
+        lengths.reshape(1, -1),
         index.reshape(1, -1),
         slots.reshape(1, -1),
         ranks.reshape(1, -1),
+        gain.reshape(1, -1),
+        stream,
+        query_weight,
+        pair_weight,
+        cache,
         down,
         up,
-        gain.reshape(1, -1),
-        stream,
         weight,
     )
 
@@ -562,6 +691,22 @@
     rank_padding = adapter_down_weight.shape[2]
     adapter_portion = adapter_up_weight.shape[2]
     capacity = row_count // 4
+    if lax.axis_size("tensor") == 4 and adapter_portion % 128 == 0 and row_count == 128:
+        return exchange(
+            stream,
+            input_norm_gain,
+            row_cache_length,
+            query_projection,
+            key_value_weight,
+            cached_key_value,
+            row_adapter_index,
+            adapter_slot_table,
+            adapter_rank_table,
+            adapter_down_weight,
+            adapter_up_weight,
+            output_norm_gain,
+            output_projection,
+        )
     mixed = attention(
         stream,
         input_norm_gain,
@@ -570,18 +715,6 @@
         key_value_weight,
         cached_key_value,
     )
-    if lax.axis_size("tensor") == 4 and adapter_portion % 128 == 0 and row_count == 128:
-        return exchange(
-            mixed,
-            row_adapter_index,
-            adapter_slot_table,
-            adapter_rank_table,
-            adapter_down_weight,
-            adapter_up_weight,
-            output_norm_gain,
-            stream,
-            output_projection,
-        )
     stream_f = stream.astype(jnp.float32)
     adapters = adapter_slot_table.shape[0]
     match = row_adapter_index[:, None] == jnp.arange(adapters)[None, :]

time: 62 us -> 62.8 us (1.013)
  Pallas kernels: 54.3 us -> 58.2 us
  local copies, waits for them, and re-layouts: 7.37 us -> 4.31 us
    pallas_call x1, Pallas kernels: 29.5 us -> 58.2 us  [exchange(): pl.pallas_call(functools.partial(exchange_kernel, stores, column_count, k...]
    pallas_call x1 -> x0, Pallas kernels: 24.8 us -> none  [attention(): pl.pallas_call(functools.partial(attention_kernel, per), out_shape=jax.Sh...]
    unnamed x17 -> x1, local copies, waits for them, and re-layouts: 5.37 us -> 1.7 us
where the time goes in v3:
time: 62.8 us; the launch traced here: 62.5 us
  Pallas kernels  58.2 us (93%)
  local copies, waits for them, and re-layouts  4.31 us (7%)
    pallas_call x1, Pallas kernels, exchange(): pl.pallas_call(functools.partial(exchange_kernel, stores, column_count, k...  58.2 us
    unnamed x1, local copies, waits for them, and re-layouts  1.7 us
    reshape x1, local copies, waits for them, and re-layouts, exchange(): input_gain.reshape(1, -1)  1.32 us
    reshape x1, local copies, waits for them, and re-layouts, exchange(): gain.reshape(1, -1)  1.29 us

profile of v3, /device:TPU:0, one launch (start us, length us, event | category | flops | bytes accessed | tf_op | source)
XLA Modules:
  0.0 62.5 jit_solution(3773297689223027374)
XLA Ops:
  0.0 1.3 %reshape.29.gain_ref = bf16[1,1152]{1,0:T(2,128)(2,1)} reshape(bf16[1152]{0:T(1024)(128)(2,1)} %param.15) | data formatting | bytes 4608 | tf_op jit(solution)/shard_map/reshape | solution.py:661
  1.3 1.3 %reshape.24.input_gain_ref = bf16[1,4608]{1,0:T(2,128)(2,1)} reshape(bf16[4608]{0:T(1024)(128)(2,1)} %param.14) | data formatting | bytes 18432 | tf_op jit(solution)/shard_map/reshape | solution.py:656
  2.6 58.2 %shard_map.127 = bf16[128,1152]{1,0:T(8,128)(2,1)} custom-call(bf16[1,4608]{1,0:T(2,128)(2,1)} %reshape.24.input_gain_ref, s32[1,128]{1,0:T(1,128)} %bitcast.10, s32[1,128]{1,0:T(1,128)} %bitcast.11, s32[1,32]{1,0:T(1,128)} %bitcast.12, s32[1,32]{1,0:T(1,128)} %bitcast.13, bf16[1,1152]{1,0:T(2,128)(2,1)} %reshape.29.gain_ref, bf16[128,4608]{1,0:T(8,128)(2,1)} %stream_ref.1, ...), custom_call_target="tpu_custom_call" | custom-call | tf_op jit(solution)/shard_map/pallas_call | solution.py:609
  60.8 1.7 %copy.15 = bf16[128,1152]{1,0:T(8,128)(2,1)} copy(bf16[128,1152]{1,0:T(8,128)(2,1)} %shard_map.127) | data formatting | bytes 589824

commit v4 on v3

--- a/solution.py
+++ b/solution.py
@@ -81,15 +81,16 @@
     stream_copy.start()
     for c in range(chunks):
         pair_copy(c).start()
-        query_copy(c).start()
+        query_copy(c).start(priority=1)
     if begin is not None:
         begin()
     stream_copy.wait()
     stream = stream_buf[...].astype(f32)
     scale = lax.rsqrt(jnp.mean(stream * stream, axis=-1, keepdims=True) + epsilon)
+    gain = gain_ref[...].astype(f32).reshape(1, width)
     for c in range(chunks):
         cut = slice(c * step, (c + 1) * step)
-        normed_buf[c] = (stream[:, cut] * scale * gain_ref[:, cut].astype(f32)).astype(bf16)
+        normed_buf[c] = (stream[:, cut] * scale * gain[:, cut]).astype(bf16)
     length = jnp.broadcast_to(length_ref[...].astype(f32), (128, rows)).T
     length_buf[...] = length
     lane = lax.broadcasted_iota(jnp.int32, (rows, 128), 1)
@@ -130,7 +131,7 @@
         @pl.when(c < slots)
         def _():
             cache_copy(0, c).start()
-            cache_copy(1, c).start()
+            cache_copy(1, c).start(priority=1)
 
         return carry
 
@@ -201,7 +202,7 @@
         @pl.when(part + slots < parts)
         def _():
             cache_copy(0, part + slots).start()
-            cache_copy(1, part + slots).start()
+            cache_copy(1, part + slots).start(priority=1)
 
         if after_group is not None:
 
@@ -255,7 +256,7 @@
         out_specs=vmem,
         scratch_shapes=attention_scratch(rows, width, query_weight, pair_weight, cache),
         compiler_params=pltpu.CompilerParams(vmem_limit_bytes=60 << 20),
-    )(stream, gain.reshape(1, -1), lengths.reshape(1, -1), query_weight, pair_weight, cache)
+    )(stream, gain, lengths.reshape(1, -1), query_weight, pair_weight, cache)
 
 
 def exchange_kernel(
@@ -314,7 +315,7 @@
     *attention_refs,
 ):
     rows, depth = mixed_ref.shape
-    portion = gain_ref.shape[1]
+    portion = gain_ref.shape[0]
     rank_width = down_ref.shape[0] // kept
     pairs = out_buf.shape[1]
     span = depth // pairs
@@ -415,8 +416,8 @@
         pl.semaphore_wait(barrier, stores + column_count - 2)
         for k in range(1, stores):
             label_copy(k).start()
-        for load in loads:
-            load.start()
+        for i, load in enumerate(loads):
+            load.start(priority=i % 2)
 
     def send_group(g):
         start = pl.multiple_of(g * span, 128)
@@ -459,20 +460,6 @@
         )
         copy.start()
         part_copies.append(copy)
-    loads[2].wait()
-    crossing = jnp.dot(mixed, weight_buf[2], preferred_element_type=f32)
-    part_copies[0].wait()
-    cross_buf[...] = (crossing + part_in[0].astype(f32)).astype(bf16)
-    cross_copy = pltpu.make_async_remote_copy(
-        src_ref=cross_buf,
-        dst_ref=cross_in,
-        send_sem=part_send.at[2],
-        recv_sem=part_recv.at[2],
-        device_id={"tensor": across},
-        device_id_type=MESH,
-    )
-    cross_copy.start()
-
     for k in range(1, stores):
         label_copy(k).wait()
     label = jnp.concatenate([label_buf[0]] + [label_in[k] for k in range(stores - 1)], axis=0)
@@ -510,6 +497,20 @@
         )
         copy.start()
         low_copies.append(copy)
+
+    loads[2].wait()
+    crossing = jnp.dot(mixed, weight_buf[2], preferred_element_type=f32)
+    part_copies[0].wait()
+    cross_buf[...] = (crossing + part_in[0].astype(f32)).astype(bf16)
+    cross_copy = pltpu.make_async_remote_copy(
+        src_ref=cross_buf,
+        dst_ref=cross_in,
+        send_sem=part_send.at[2],
+        recv_sem=part_recv.at[2],
+        device_id={"tensor": across},
+        device_id_type=MESH,
+    )
+    cross_copy.start()
 
     loads[3].wait()
     own = jnp.dot(mixed, weight_buf[3], preferred_element_type=f32)
@@ -569,7 +570,8 @@
     total = jnp.broadcast_to(total, (128, rows)).T[:, 0:1]
     factor = lax.rsqrt(total * (1.0 / width) + epsilon)
     out_ref[...] = (
-        stream_buf[...].astype(f32) + projected * factor * gain_ref[...].astype(f32)
+        stream_buf[...].astype(f32)
+        + projected * factor * gain_ref[...].astype(f32).reshape(1, portion)
     ).astype(bf16)
 
 
@@ -653,12 +655,12 @@
             collective_id=0, has_side_effects=True, vmem_limit_bytes=62 << 20
         ),
     )(
-        input_gain.reshape(1, -1),
+        input_gain,
         lengths.reshape(1, -1),
         index.reshape(1, -1),
         slots.reshape(1, -1),
         ranks.reshape(1, -1),
-        gain.reshape(1, -1),
+        gain,
         stream,
         query_weight,
         pair_weight,

time: 62.8 us -> 53.4 us (0.85)
  Pallas kernels: 58.2 us -> 51.5 us
  local copies, waits for them, and re-layouts: 4.31 us -> 1.7 us
    pallas_call x1, Pallas kernels: 58.2 us -> 51.5 us  [exchange(): pl.pallas_call(functools.partial(exchange_kernel, stores, column_count, k...]
    reshape x2 -> x0, local copies, waits for them, and re-layouts: 2.61 us -> none  [the longest x1 1.32 us: exchange(): input_gain.reshape(1, -1)]
where the time goes in v4:
time: 53.4 us; the launch traced here: 53.3 us
  Pallas kernels  51.5 us (96%)
  local copies, waits for them, and re-layouts  1.7 us (3%)
    pallas_call x1, Pallas kernels, exchange(): pl.pallas_call(functools.partial(exchange_kernel, stores, column_count, k...  51.5 us
    unnamed x1, local copies, waits for them, and re-layouts  1.7 us

profile of v4, /device:TPU:0, one launch (start us, length us, event | category | flops | bytes accessed | tf_op | source)
XLA Modules:
  0.0 53.3 jit_solution(11200780401551502570)
XLA Ops:
  0.0 51.5 %shard_map.127 = bf16[128,1152]{1,0:T(8,128)(2,1)} custom-call(bf16[4608]{0:T(1024)(128)(2,1)} %input_gain_ref.1, s32[1,128]{1,0:T(1,128)} %bitcast.10, s32[1,128]{1,0:T(1,128)} %bitcast.11, s32[1,32]{1,0:T(1,128)} %bitcast.12, s32[1,32]{1,0:T(1,128)} %bitcast.13, bf16[1152]{0:T(1024)(128)(2,1)} %gain_ref.1, bf16[128,4608]{1,0:T(8,128)(2,1)} %stream_ref.1, ...), custom_call_target="tpu_custom_call" | custom-call | tf_op jit(solution)/shard_map/pallas_call | solution.py:611
  51.6 1.7 %copy.15 = bf16[128,1152]{1,0:T(8,128)(2,1)} copy(bf16[128,1152]{1,0:T(8,128)(2,1)} %shard_map.127) | data formatting | bytes 589824
